TPU v7x, 512 devices: a whole 4x8x8 slice. The times are simulated.
512 devices in a mesh: lists: 128 (over y, z, core), rep: 4 (over x).
Axes of the slice: x: 4, y: 8, z: 8, core: 2. Of those that a mesh axis runs over, the one named last changes fastest.
Arguments:
- vector_codes: bfloat16 [65536, 1024], P(('lists', 'rep')), may hold values from -6 to 6
- row_scales: bfloat16 [65536], P(('lists', 'rep')), may hold values from 0.29882812 to 3
- old_list: int32 [65536], P(('lists', 'rep')), may hold values from 0 to 65535, as said below
- new_list: int32 [65536], P(('lists', 'rep')), may hold values from 0 to 65535, as said below
- pq_codes: int32 [65536, 64], P(('lists', 'rep')), may hold values from 0 to 255
- centroids: bfloat16 [65536, 1024], P('lists'), may hold values from -6 to 6
Outputs:
- centroid_delta: bfloat16 [65536, 1024], P('lists', 'rep')
- codebook_sums: float32 [64, 4096], P('rep')
Inputs may be any that keep to these rules, and one draw needn't show every extreme that they name: `old_list`: every row held by the device at lists index i names a list from i * 512 to (i + 1) * 512 - 1. `new_list`: the owner of list l is lists index l // 512. Among the rows of one device at most 2 name lists of one owner, and in every draw one owner is named by exactly 2 rows of every device.
All inputs are finite; a program needn't handle non-finite values.
Results may differ from a plain program's by a relative error of at most 0.009.
Values may be sent and summed in bfloat16 or wider, within the bound.
A program may use at most 64 MiB of HBM per device.

v0:
```python
import jax
import jax.numpy as jnp
from jax import lax
from jax.sharding import PartitionSpec as P

M = 64
KSUB = 256


def body(vector_codes, row_scales, old_list, new_list, pq_codes, centroids):
    num_lists = lax.axis_size("lists")
    owner_index = lax.axis_index("lists")
    local_rows = vector_codes.shape[0]
    full_width = vector_codes.shape[1]
    list_count = centroids.shape[0]
    sub_width = full_width // M
    capacity = 2 * local_rows // num_lists
    block_count = 1
    total_rows = block_count * local_rows
    sub_local = pq_codes.shape[1]
    owners = new_list // list_count
    owner_hits = (owners[:, None] == jnp.arange(num_lists, dtype=jnp.int32)[None, :]).astype(
        jnp.int32
    )
    owner_hits = owner_hits.reshape(block_count, local_rows, num_lists)
    slot_ranks = jnp.sum(owner_hits * (jnp.cumsum(owner_hits, axis=1) - 1), axis=2).reshape(-1)
    block_of = jnp.arange(total_rows, dtype=jnp.int32) // local_rows
    slot_depth = block_count * capacity
    target = owners * slot_depth + block_of * capacity + slot_ranks
    source_of = jnp.full((num_lists * slot_depth,), total_rows, jnp.int32)
    source_of = source_of.at[target].set(jnp.arange(total_rows, dtype=jnp.int32))
    padded_codes = jnp.concatenate([vector_codes, jnp.zeros((1, full_width), jnp.bfloat16)], axis=0)
    padded_scales = jnp.concatenate([row_scales, jnp.zeros((1,), jnp.bfloat16)], axis=0)
    padded_ids = jnp.concatenate([new_list, jnp.full((1,), -1, jnp.int32)], axis=0)
    padded_pq = jnp.concatenate([pq_codes, jnp.zeros((1, sub_local), jnp.int32)], axis=0)
    send_codes = jnp.take(padded_codes, source_of, axis=0).reshape(
        num_lists, slot_depth, full_width
    )
    send_scales = jnp.take(padded_scales, source_of, axis=0).reshape(num_lists, slot_depth)
    send_ids = jnp.take(padded_ids, source_of, axis=0).reshape(num_lists, slot_depth)
    send_pq = jnp.take(padded_pq, source_of, axis=0).reshape(num_lists, slot_depth, sub_local)
    got_codes, got_scales = (
        lax.all_to_all(send_codes, "lists", split_axis=0, concat_axis=0, tiled=True),
        lax.all_to_all(send_scales, "lists", split_axis=0, concat_axis=0, tiled=True),
    )
    got_ids, got_pq = (
        lax.all_to_all(send_ids, "lists", split_axis=0, concat_axis=0, tiled=True),
        lax.all_to_all(send_pq, "lists", split_axis=0, concat_axis=0, tiled=True),
    )
    recv_rows = num_lists * slot_depth
    got_codes = got_codes.reshape(recv_rows, full_width)
    got_scales = got_scales.reshape(recv_rows)
    got_ids = got_ids.reshape(recv_rows)
    got_pq = got_pq.reshape(recv_rows, sub_local)
    filled = got_ids >= 0
    local_ids = jnp.where(filled, got_ids - owner_index * list_count, 0)
    list_range = jnp.arange(list_count, dtype=jnp.int32)
    new_weight = jnp.where(
        (list_range[:, None] == local_ids[None, :]) & filled[None, :],
        got_scales[None, :],
        jnp.zeros((), jnp.bfloat16),
    )
    new_sum = jnp.dot(new_weight, got_codes, preferred_element_type=jnp.float32)
    old_local = old_list - owner_index * list_count
    old_weight = jnp.where(
        list_range[:, None] == old_local[None, :], row_scales[None, :], jnp.zeros((), jnp.bfloat16)
    )
    old_sum = jnp.dot(old_weight, vector_codes, preferred_element_type=jnp.float32)
    partial_value = new_sum - old_sum
    values = got_codes.astype(jnp.float32) * got_scales.astype(jnp.float32)[:, None]
    nearest = jnp.take(centroids, local_ids, axis=0).astype(jnp.float32)
    residual = (values - nearest).astype(jnp.bfloat16)
    group_size = min(128 // sub_width, sub_local)
    code_range = jnp.arange(KSUB, dtype=jnp.int32)
    diag_index = jnp.arange(group_size)
    results = []
    for first_sub in range(0, sub_local, group_size):
        code_picks = got_pq[0:recv_rows, first_sub : first_sub + group_size]
        code_hits = (code_picks[:, :, None] == code_range[None, None, :]) & filled[:, None, None]
        code_hits = code_hits.astype(jnp.bfloat16).reshape(recv_rows, group_size * KSUB)
        columns = residual[
            0:recv_rows, first_sub * sub_width : (first_sub + group_size) * sub_width
        ]
        group_total = lax.dot_general(
            code_hits, columns, (((0,), (0,)), ((), ())), preferred_element_type=jnp.float32
        )
        diagonal = group_total.reshape(group_size, KSUB, group_size, sub_width)[
            diag_index, :, diag_index, :
        ]
        results.append(diagonal.reshape(group_size, KSUB * sub_width))
    codebook_part = jnp.concatenate(results, axis=0)
    list_delta = lax.psum_scatter(partial_value, "rep", scatter_dimension=1, tiled=True)
    codebook = lax.psum_scatter(
        codebook_part.astype(jnp.bfloat16), "rep", scatter_dimension=0, tiled=True
    ).astype(jnp.float32)
    codebook = lax.psum(codebook, "lists")
    return (list_delta.astype(jnp.bfloat16), codebook)


def solution(mesh):
    return jax.shard_map(
        body,
        mesh=mesh,
        in_specs=(
            P(("lists", "rep"), None),
            P(("lists", "rep")),
            P(("lists", "rep")),
            P(("lists", "rep")),
            P(("lists", "rep"), None),
            P("lists", None),
        ),
        out_specs=(P("lists", "rep"), P("rep", None)),
        check_vma=False,
    )
```

profile of v0, /device:TPU:1, one launch (start us, length us, event | category | flops | bytes accessed | tf_op | source)
XLA Modules:
  0.0 686.8 jit_solution(5561019028925906111)
XLA Ops:
  10.8 1.9 gather_fusion.1
  13.5 18.4 %all-to-all-start.1 = ((bf16[128,1,2]{2,1,0:T(2,128)(2,1)}), bf16[128,1,2]{2,1,0:T(2,128)(2,1)S(1)}, u32[]{:S(2)}, u32[]{:S(2)}) async-start(bf16[128,1,2]{2,1,0:T(2,128)(2,1)} %select_n.145), calls=%async_computation.1 | async-start | bytes 131072 | tf_op jit(solution)/shard_map/all_to_all | solution.py:44
  32.5 1.9 gather_fusion
  39.1 4.2 all-to-all-done.1
  43.3 9.5 %all-to-all-start = ((s32[128,1,2]{2,1,0:T(1,128)}), s32[128,1,2]{2,1,0:T(1,128)S(1)}, u32[]{:S(2)}, u32[]{:S(2)}) async-start(s32[128,1,2]{2,1,0:T(1,128)} %bitcast), calls=%async_computation | async-start | bytes 131072 | tf_op jit(solution)/shard_map/all_to_all | solution.py:47
  53.8 10.5 %all-to-all-done = s32[128,1,2]{2,1,0:T(1,128)S(1)} async-done(((s32[128,1,2]{2,1,0:T(1,128)}), s32[128,1,2]{2,1,0:T(1,128)S(1)}, u32[]{:S(2)}, u32[]{:S(2)}) %all-to-all-start) | async-done | bytes 1056 | tf_op jit(solution)/shard_map/all_to_all | solution.py:47
  64.3 5.7 all-to-all-start.3
  70.4 11.2 %all-to-all-done.3 = s32[128,1,128]{2,1,0:T(1,128)S(1)} async-done(((s32[128,1,128]{2,1,0:T(1,128)}), s32[128,1,128]{2,1,0:T(1,128)S(1)}, u32[]{:S(2)}, u32[]{:S(2)}) %all-to-all-start.3) | async-done | bytes 65568 | tf_op jit(solution)/shard_map/all_to_all | solution.py:48
  81.6 6.9 %all-to-all-start.2 = ((bf16[128,2,1024]{2,1,0:T(2,128)(2,1)}), bf16[128,2,1024]{2,1,0:T(2,128)(2,1)}, u32[]{:S(2)}, u32[]{:S(2)}) async-start(bf16[128,2,1024]{2,1,0:T(2,128)(2,1)} %broadcast_select_fusion), calls=%async_computation.2 | async-start | bytes 1048576 | tf_op jit(solution)/shard_map/all_to_all | solution.py:43
  93.2 4.5 fusion.7
  97.7 10.1 %all-to-all-done.2 = bf16[128,2,1024]{2,1,0:T(2,128)(2,1)} async-done(((bf16[128,2,1024]{2,1,0:T(2,128)(2,1)}), bf16[128,2,1024]{2,1,0:T(2,128)(2,1)}, u32[]{:S(2)}, u32[]{:S(2)}) %all-to-all-start.2) | async-done | bytes 524320 | tf_op jit(solution)/shard_map/all_to_all | solution.py:43
  121.1 2.4 fusion.38
  129.0 2.4 reshape.318
  132.4 1.8 reshape.324
  134.3 2.3 fusion.33
  139.2 2.4 reshape.319
  141.6 2.1 fusion.34
  146.4 2.5 reshape.320
  148.9 2.3 fusion.35
  153.8 2.4 reshape.321
  156.2 2.1 fusion.36
  168.3 1.8 convolution_subtract_fusion
  170.2 16.6 %reduce-scatter.5.cloned.1.call-done = bf16[16,4096]{1,0:T(8,128)(2,1)} async-done(((bf16[64,4096]{1,0:T(8,128)(2,1)}), bf16[16,4096]{1,0:T(8,128)(2,1)}) %reduce-scatter.5.cloned.1.call-update) | async-done | bytes 131088 | tf_op jit(solution)/shard_map/reduce_scatter | solution.py:93
  186.7 491.5 %all-reduce.3 = f32[16,4096]{1,0:T(8,128)} all-reduce(bf16[16,4096]{1,0:T(8,128)(2,1)} %reduce-scatter.5.cloned.1.call-done), channel_id=1, replica_groups=mesh['lists'=128,'rep'=4] {'lists'}, use_global_device_ids=true, to_apply=%region_5.6 | all-reduce | flops 65536 | bytes 393216 | tf_op jit(solution)/shard_map/psum | solution.py:96
  (135 shorter events, 54.6 us)
Async XLA Ops:
  7.2 82.5 %copy-start = (bf16[512,1024]{1,0:T(8,128)(2,1)S(1)}, bf16[512,1024]{1,0:T(8,128)(2,1)}, u32[]{:S(2)}) copy-start(bf16[512,1024]{1,0:T(8,128)(2,1)} %param.11) | copy-start | bytes 3145732
  7.2 27.5 %copy-start.4 = (bf16[128,1024]{1,0:T(8,128)(2,1)S(1)}, bf16[128,1024]{1,0:T(8,128)(2,1)}, u32[]{:S(2)}) copy-start(bf16[128,1024]{1,0:T(8,128)(2,1)} %param.6) | copy-start | bytes 786436
  13.5 29.9 %all-to-all-start.1 = ((bf16[128,1,2]{2,1,0:T(2,128)(2,1)}), bf16[128,1,2]{2,1,0:T(2,128)(2,1)S(1)}, u32[]{:S(2)}, u32[]{:S(2)}) async-start(bf16[128,1,2]{2,1,0:T(2,128)(2,1)} %select_n.145), calls=%async_computation.1 | async-start | bytes 131072 | tf_op jit(solution)/shard_map/all_to_all | solution.py:44
  35.9 2.4 copy-start.14
  43.3 21.0 %all-to-all-start = ((s32[128,1,2]{2,1,0:T(1,128)}), s32[128,1,2]{2,1,0:T(1,128)S(1)}, u32[]{:S(2)}, u32[]{:S(2)}) async-start(s32[128,1,2]{2,1,0:T(1,128)} %bitcast), calls=%async_computation | async-start | bytes 131072 | tf_op jit(solution)/shard_map/all_to_all | solution.py:47
  64.3 17.3 %all-to-all-start.3 = ((s32[128,1,128]{2,1,0:T(1,128)}), s32[128,1,128]{2,1,0:T(1,128)S(1)}, u32[]{:S(2)}, u32[]{:S(2)}) async-start(s32[128,1,128]{2,1,0:T(1,128)} %reshape.458), calls=%async_computation.4 | async-start | bytes 131072 | tf_op jit(solution)/shard_map/all_to_all | solution.py:48
  81.6 26.1 %all-to-all-start.2 = ((bf16[128,2,1024]{2,1,0:T(2,128)(2,1)}), bf16[128,2,1024]{2,1,0:T(2,128)(2,1)}, u32[]{:S(2)}, u32[]{:S(2)}) async-start(bf16[128,2,1024]{2,1,0:T(2,128)(2,1)} %broadcast_select_fusion), calls=%async_computation.2 | async-start | bytes 1048576 | tf_op jit(solution)/shard_map/all_to_all | solution.py:43
  88.5 98.2 %reduce-scatter.5.cloned.1.call-start = ((), (), s32[]{:S(2)}) async-start(), calls=%async_computation.7 | async-start | bytes 655360 | tf_op jit(solution)/shard_map/reduce_scatter | solution.py:93
  109.3 15.8 %copy-start.3 = (pred[256,2048]{0,1:T(32,128)(4,1)S(1)}, pred[256,2048]{0,1:T(32,128)(4,1)}, u32[]{:S(2)}) copy-start(pred[256,2048]{0,1:T(32,128)(4,1)} %get-tuple-element.25) | copy-start | bytes 1572868
  121.1 4.0 copy-start.13
  132.4 9.2 %copy-start.2 = (pred[256,2048]{0,1:T(32,128)(4,1)S(1)}, pred[256,2048]{0,1:T(32,128)(4,1)}, u32[]{:S(2)}) copy-start(pred[256,2048]{0,1:T(32,128)(4,1)} %get-tuple-element.27) | copy-start | bytes 1572868
  139.2 9.7 %copy-start.9 = (bf16[128,256]{1,0:T(8,128)(2,1)S(1)}, bf16[128,256]{1,0:T(8,128)(2,1)}, u32[]{:S(2)}) copy-start(bf16[128,256]{1,0:T(8,128)(2,1)} %copy.66) | copy-start | bytes 196612
  146.4 9.8 %copy-start.1 = (pred[256,2048]{0,1:T(32,128)(4,1)S(1)}, pred[256,2048]{0,1:T(32,128)(4,1)}, u32[]{:S(2)}) copy-start(pred[256,2048]{0,1:T(32,128)(4,1)} %get-tuple-element.29) | copy-start | bytes 1572868
  161.6 3.1 copy-start.6
  163.9 3.0 copy-start.7
  163.9 3.0 copy-start.8
  163.9 3.0 copy-start.10
  163.9 3.0 copy-start.11
  164.7 2.3 copy-start.12
  165.2 2.7 copy-start.16
  165.2 2.7 copy-start.15
  167.0 0.8 copy-start.5
  167.8 510.4 %reduce-scatter.3.cloned.1.call-start = ((), (), s32[]{:S(2)}) async-start(), calls=%async_computation.6 | async-start | bytes 2621440 | tf_op jit(solution)/shard_map/reduce_scatter | solution.py:92
Sparse Core Ops, SparseCore 0:
  168.0 18.7 reduce-scatter.4
  189.6 36.4 reduce-scatter.2
where the time goes:
time: 692 us; the launch traced here: 687 us
  blocking collectives  491 us (71%)
  local copies, waits for them, and re-layouts  57.8 us (8%)
  waiting for transfers between devices  52.6 us (8%)
  starting transfers between devices  40.6 us (6%)
  matrix products  16.6 us (2%)
  between operations  14.7 us (2%)
  other arithmetic  13 us (2%)
    psum x1, blocking collectives, body(): codebook = lax.psum(codebook, 'lists')  491 us
    all_to_all x1, starting transfers between devices, body(): lax.all_to_all(send_scales, 'lists', split_axis=0, concat_axis=0, tiled=T...  18.4 us
    reduce_scatter x1, waiting for transfers between devices, body(): lax.psum_scatter(codebook_part.astype(jnp.bfloat16), 'rep', scatter_dimen...  16.6 us
    reshape x8, local copies, waits for them, and re-layouts, body(): results.append(diagonal.reshape(group_size, KSUB * sub_width))  14.5 us
    dot_general x8, matrix products, body(): lax.dot_general(code_hits, columns, (((0,), (0,)), ((), ())), preferred_e...  14.4 us
  transfers between devices with their start and end apart: 6, of which 5 were waited for; matrix products, arithmetic and copies ran while one was open for 3% of the time, Pallas kernels for 0%

commit v1 on v0

v1 whole, which is shorter than its diff:
```python
import functools

import jax
import jax.numpy as jnp
from jax import lax
from jax.experimental import pallas as pl
from jax.experimental.pallas import tpu as pltpu
from jax.sharding import PartitionSpec as P

MESH = pl.DeviceIdType.MESH
F32 = jnp.float32
BF16 = jnp.bfloat16
I32 = jnp.int32

N_LISTS = 128
N_REP = 4
CHIPS = N_LISTS // 2
ROWS = 128
GROUP = ROWS * N_REP
LISTS = 512
COLS = 256
SLOTS = 8
KK = 16
KSUB = 256
NT = (((1,), (1,)), ((), ()))
NN = (((1,), (0,)), ((), ()))


def dot(a, b, dims=NN):
    return lax.dot_general(a, b, dims, preferred_element_type=F32)


def iota(shape, axis):
    return lax.broadcasted_iota(I32, shape, axis)


def chip_at(chip, step):
    off = lax.rem(step * 27, CHIPS)
    y = lax.rem(chip // 8 + off // 8, 8)
    z = lax.rem(lax.rem(chip, 8) + lax.rem(off, 8), 8)
    return y * 8 + z


def list_peer(me, step):
    off = lax.rem(step * 53, N_LISTS)
    y = lax.rem(me // 16 + off // 16, 8)
    z = lax.rem(lax.rem(me // 2, 8) + lax.rem(off // 2, 8), 8)
    c = lax.rem(lax.rem(me, 2) + lax.rem(off, 2), 2)
    return (y * 8 + z) * 2 + c


def kernel(
    codes,
    scale_ref,
    old_ref,
    new_ref,
    pq_ref,
    cent_hbm,
    delta_out,
    book_out,
    cent,
    xbuf,
    msend,
    mrecv,
    esend,
    erecv,
    vsend,
    vrecv,
    delta_acc,
    vflat,
    pqk,
    centg,
    book,
    sib,
    comb,
    rsbuf,
    tile,
    gathered,
    cent_sem,
    loc_sem,
    xs_sem,
    xr_sem,
    ms_sem,
    mr_sem,
    es_sem,
    er_sem,
    vs_sem,
    vr_sem,
    bs_sem,
    br_sem,
    rs_sem,
    rr_sem,
    ts_sem,
    tr_sem,
    gs_sem,
    gr_sem,
):
    me = lax.axis_index("lists")
    rep = lax.axis_index("rep")
    core = lax.rem(me, 2)
    chip = me // 2
    sibling = me + 1 - 2 * core

    def copy_to(src, dst, ssem, rsem, **device):
        return pltpu.make_async_remote_copy(
            src, dst, ssem, rsem, device_id=device, device_id_type=MESH
        )

    cent_copy = pltpu.make_async_copy(
        cent_hbm.at[:, pl.ds(pl.multiple_of(rep * COLS, COLS), COLS)], cent, cent_sem
    )
    cent_copy.start()

    barrier = pltpu.get_barrier_semaphore()
    for k in range(1, N_REP):
        pl.semaphore_signal(
            barrier, inc=1, device_id={"rep": lax.rem(rep + k, N_REP)}, device_id_type=MESH
        )

    def greet(k, carry):
        pl.semaphore_signal(
            barrier, inc=1, device_id={"lists": list_peer(me, k)}, device_id_type=MESH
        )
        return carry

    lax.fori_loop(1, N_LISTS, greet, 0)

    scale = scale_ref[...].astype(F32)
    new = new_ref[...]
    owner = new // LISTS
    new_in = new - owner * LISTS + 1
    old_in = old_ref[...] - me * LISTS
    own_row = jnp.broadcast_to(owner.astype(F32), (ROWS, ROWS))
    own_col = jnp.transpose(own_row)
    earlier = (own_row == own_col) & (iota((ROWS, ROWS), 0) < iota((ROWS, ROWS), 1))
    rank = jnp.sum(jnp.where(earlier, 1.0, 0.0), axis=0, keepdims=True)
    target = owner.astype(F32) * 2.0 + rank
    new_hi = new_in // 256
    old_hi = old_in // 256
    shape = (N_REP * 32, 64)
    line = iota(shape, 0)
    pick = (line // 32) * 16 + 2 * lax.rem(line, 16) + lax.rem(line, 32) // 16
    pick = jnp.where(lax.rem(line, 16) < 8, pick, -1)
    chooser = jnp.where(pick == iota(shape, 1), 1.0, 0.0).astype(BF16)
    meta = dot(chooser, pq_ref[...].astype(F32).astype(BF16), NT)
    line = lax.rem(iota((N_REP * 32, ROWS), 0), 32)
    extra = (
        (8, (new_in - new_hi * 256).astype(F32)),
        (24, new_hi.astype(F32)),
        (9, scale),
        (10, target),
        (11, (old_in - old_hi * 256).astype(F32)),
        (27, old_hi.astype(F32)),
    )
    for at, row in extra:
        meta = jnp.where(line == at, row, meta)
    msend[...] = meta.astype(BF16).reshape(N_REP, 32, ROWS)

    pl.semaphore_wait(barrier, N_LISTS - 1 + N_REP - 1)

    for k in range(1, N_REP):
        peer = lax.rem(rep + k, N_REP)
        copy_to(msend.at[peer], mrecv.at[rep], ms_sem, mr_sem, rep=peer).start()
    for k in range(1, N_REP):
        peer = lax.rem(rep + k, N_REP)
        copy_to(
            codes.at[:, pl.ds(pl.multiple_of(peer * COLS, COLS), COLS)],
            xbuf.at[rep],
            xs_sem,
            xr_sem,
            rep=peer,
        ).start()
    own = pltpu.make_async_copy(
        codes.at[:, pl.ds(pl.multiple_of(rep * COLS, COLS), COLS)], xbuf.at[rep], loc_sem
    )
    own.start()
    mrecv[rep] = msend[rep]
    peer = lax.rem(rep + 1, N_REP)
    three = mrecv.at[pl.ds(0, N_REP - 1)]
    wait = copy_to(three, three, ms_sem, mr_sem, rep=peer)
    wait.wait_recv()
    wait.wait_send()

    low = jnp.concatenate([mrecv[s, 0:16, :] for s in range(N_REP)], axis=1).astype(F32)
    high = jnp.concatenate([mrecv[s, 16:32, :] for s in range(N_REP)], axis=1).astype(F32)
    target = low[10:11, :].astype(I32)
    owner = target // 2
    slot = (iota((1, GROUP), 1) // ROWS) * 2 + target - owner * 2
    at_owner = jnp.where(iota((N_LISTS, GROUP), 0) == owner, 1.0, 0.0).astype(BF16)
    slot_b = jnp.broadcast_to(slot, (KK, GROUP))
    low_s = jnp.concatenate([jnp.where(slot_b == q, low, 0.0) for q in range(SLOTS)], axis=0)
    high_s = jnp.concatenate([jnp.where(slot_b == q, high, 0.0) for q in range(SLOTS)], axis=0)
    routed = dot(at_owner, low_s.astype(BF16), NT) + 256.0 * dot(
        at_owner, high_s.astype(BF16), NT
    )
    esend[...] = routed.reshape(N_LISTS, 1, SLOTS * KK)

    def send_meta(k, carry):
        peer = list_peer(me, k)
        copy_to(esend.at[peer], erecv.at[me], es_sem, er_sem, lists=peer).start()
        return carry

    lax.fori_loop(1, N_LISTS, send_meta, 0)
    erecv[me] = esend[me]

    own.wait()
    three = xbuf.at[pl.ds(0, N_REP - 1)]
    wait = copy_to(three, three, xs_sem, xr_sem, rep=peer)
    wait.wait_recv()
    wait.wait_send()
    place = owner * SLOTS + slot
    x = xbuf[...].reshape(GROUP, COLS)
    move = jnp.where(iota((N_LISTS * SLOTS, GROUP), 0) == place, 1.0, 0.0).astype(BF16)
    moved = dot(move, x).reshape(N_LISTS, SLOTS, COLS)
    vsend[...] = jnp.concatenate([moved[:, :, 0:128], moved[:, :, 128:256]], axis=1).astype(BF16)

    def send_vec(k, carry):
        peer = list_peer(me, k)
        copy_to(vsend.at[peer], vrecv.at[me], vs_sem, vr_sem, lists=peer).start()
        return carry

    lax.fori_loop(1, N_LISTS, send_vec, 0)
    vrecv[me] = vsend[me]

    scale = low[9:10, :]
    old_in = low[11:12, :] + 256.0 * high[11:12, :]
    weight = jnp.where(iota((LISTS, GROUP), 0).astype(F32) == old_in, scale, 0.0).astype(BF16)
    delta_acc[...] = dot(weight, x)
    pqk[0:8, 0:GROUP] = low[0:8, :]
    pqk[8:16, 0:GROUP] = high[0:8, :]
    code = iota((KSUB, GROUP), 0).astype(F32)
    lane_sub = iota((KSUB, 128), 1) // 16

    def value_sums(i, carry):
        sub = 2 * lax.rem(i, 8) + i // 8
        half = sub // 8
        hits = jnp.where(code == pqk[pl.ds(i, 1), 0:GROUP], scale, 0.0).astype(BF16)
        cols = xbuf[:, :, pl.ds(pl.multiple_of(half * 128, 128), 128)].reshape(GROUP, 128)
        total = dot(hits, cols)
        at = pl.ds(pl.multiple_of(half * KSUB, KSUB), KSUB)
        book[at, :] = jnp.where(lane_sub == lax.rem(sub, 8), total, book[at, :])
        return carry

    book[...] = jnp.zeros_like(book)
    lax.fori_loop(0, 16, value_sums, 0)

    cent_copy.wait()
    eye = jnp.where(iota((COLS, COLS), 0) == iota((COLS, COLS), 1), 1.0, 0.0).astype(BF16)
    cent_t = dot(eye, cent[...], NT).astype(BF16)

    most = erecv.at[pl.ds(0, N_LISTS - 1)]
    wait = copy_to(most, most, es_sem, er_sem, lists=sibling)
    wait.wait_recv()
    wait.wait_send()
    got = jnp.transpose(erecv[...].reshape(N_LISTS, SLOTS * KK))
    new_rows = []
    scale_rows = []
    for q in range(SLOTS):
        pairs = got[q * KK : q * KK + 8, :]
        odd = jnp.floor(pairs * (1.0 / 256.0))
        pqk[0:8, q * 128 : (q + 1) * 128] = pairs - 256.0 * odd
        pqk[8:16, q * 128 : (q + 1) * 128] = odd
        new_rows.append(got[q * KK + 8 : q * KK + 9, :])
        scale_rows.append(got[q * KK + 9 : q * KK + 10, :])
    new_in = jnp.concatenate(new_rows, axis=1) - 1.0
    new_scale = jnp.concatenate(scale_rows, axis=1)
    inside = iota((LISTS, N_LISTS * SLOTS), 0).astype(F32) == new_in
    centg[...] = dot(cent_t, jnp.where(inside, 1.0, 0.0).astype(BF16)).astype(BF16)
    code = iota((KSUB, N_LISTS * SLOTS), 0).astype(F32)

    def cent_sums(i, carry):
        sub = 2 * lax.rem(i, 8) + i // 8
        half = sub // 8
        hits = jnp.where(code == pqk[pl.ds(i, 1), :], 1.0, 0.0).astype(BF16)
        total = dot(hits, centg[pl.ds(pl.multiple_of(half * 128, 128), 128), :], NT)
        at = pl.ds(pl.multiple_of(half * KSUB, KSUB), KSUB)
        book[at, :] = book[at, :] - jnp.where(lane_sub == lax.rem(sub, 8), total, 0.0)
        return carry

    lax.fori_loop(0, 16, cent_sums, 0)
    comb[...] = book[...].reshape(CHIPS // 2, 2, 8, 128)

    pair = copy_to(comb.at[:, 1 - core], sib, bs_sem, br_sem, lists=sibling)
    pair.start()
    pair.wait()
    sib[...] = sib[...] + comb[:, core]

    def send_tile(q, carry):
        there = 2 * q + core

        @pl.when(there != chip)
        def _():
            copy_to(
                sib.at[q], rsbuf.at[chip], rs_sem, rr_sem, lists=2 * there + core
            ).start()

        return carry

    lax.fori_loop(0, CHIPS // 2, send_tile, 0)
    sums_here = lax.rem(chip, 2) == core

    @pl.when(sums_here)
    def _():
        rsbuf[chip] = sib[chip // 2]
        most = rsbuf.at[pl.ds(0, CHIPS - 1)]
        copy_to(most, most, rs_sem, rr_sem, lists=sibling).wait_recv()
        total = jnp.sum(rsbuf[...], axis=0)
        shift = lax.rem(iota((8, 128), 1) // 16 - iota((8, 128), 0) + 8, 8)
        turned = total
        for d in range(1, 8):
            moved = pltpu.roll(pltpu.roll(total, 8 - d, 0), 16 * d, 1)
            turned = jnp.where(shift == d, moved, turned)
        tile[...] = turned
        give = copy_to(tile, tile, ts_sem, tr_sem, lists=sibling)
        give.start()
        give.wait_send()
        most = sib.at[pl.ds(0, CHIPS // 2 - 1)]
        copy_to(most, most, rs_sem, rr_sem, lists=sibling).wait_send()

    @pl.when(jnp.logical_not(sums_here))
    def _():
        copy_to(tile, tile, ts_sem, tr_sem, lists=sibling).wait_recv()
        copy_to(sib, sib, rs_sem, rr_sem, lists=sibling).wait_send()

    def send_sum(k, carry):
        there = chip_at(chip, k)
        copy_to(tile, gathered.at[chip], gs_sem, gr_sem, lists=2 * there + core).start()
        return carry

    lax.fori_loop(1, CHIPS, send_sum, 0)
    gathered[chip] = tile[...]

    most = vrecv.at[pl.ds(0, N_LISTS - 1)]
    wait = copy_to(most, most, vs_sem, vr_sem, lists=sibling)
    wait.wait_recv()
    wait.wait_send()
    vflat[...] = vrecv[...].astype(F32).reshape(N_LISTS * 16, 128)
    vecs = jnp.concatenate(
        [
            jnp.concatenate(
                [vflat[pl.ds(h * 8 + q, N_LISTS, stride=16), :].astype(BF16) for h in range(2)],
                axis=1,
            )
            for q in range(SLOTS)
        ],
        axis=0,
    )
    weight = jnp.where(inside, new_scale, 0.0).astype(BF16)
    delta_out[...] = (dot(weight, vecs) - delta_acc[...]).astype(BF16)

    most = gathered.at[pl.ds(0, CHIPS - 1)]
    wait = copy_to(most, most, gs_sem, gr_sem, lists=sibling)
    wait.wait_recv()
    wait.wait_send()
    for t in range(CHIPS):
        half, block = t // 32, t % 32
        book_out[half * 8 : half * 8 + 8, block * 128 : (block + 1) * 128] = gathered[t]


def body(vector_codes, row_scales, old_list, new_list, pq_codes, centroids):
    vmem = pl.BlockSpec(memory_space=pltpu.VMEM)
    return pl.pallas_call(
        kernel,
        name="rebuild_window",
        out_shape=(
            jax.ShapeDtypeStruct((LISTS, COLS), BF16),
            jax.ShapeDtypeStruct((16, 4096), F32),
        ),
        in_specs=[vmem] * 5 + [pl.BlockSpec(memory_space=pl.ANY)],
        out_specs=(vmem, vmem),
        scratch_shapes=[
            pltpu.VMEM((LISTS, COLS), BF16),
            pltpu.VMEM((N_REP, ROWS, COLS), BF16),
            pltpu.VMEM((N_REP, 32, ROWS), BF16),
            pltpu.VMEM((N_REP, 32, ROWS), BF16),
            pltpu.VMEM((N_LISTS, 1, 128), F32),
            pltpu.VMEM((N_LISTS, 1, 128), F32),
            pltpu.VMEM((N_LISTS, 16, 128), BF16),
            pltpu.VMEM((N_LISTS, 16, 128), BF16),
            pltpu.VMEM((LISTS, COLS), F32),
            pltpu.VMEM((N_LISTS * 16, 128), F32),
            pltpu.VMEM((16, N_LISTS * SLOTS), F32),
            pltpu.VMEM((COLS, N_LISTS * SLOTS), BF16),
            pltpu.VMEM((2 * KSUB, 128), F32),
            pltpu.VMEM((CHIPS // 2, 8, 128), F32),
            pltpu.VMEM((CHIPS // 2, 2, 8, 128), F32),
            pltpu.VMEM((CHIPS, 8, 128), F32),
            pltpu.VMEM((8, 128), F32),
            pltpu.VMEM((CHIPS, 8, 128), F32),
        ]
        + [pltpu.SemaphoreType.DMA] * 18,
        compiler_params=pltpu.CompilerParams(
            collective_id=0, has_side_effects=True, vmem_limit_bytes=48 * 1024 * 1024
        ),
    )(
        vector_codes,
        row_scales.reshape(1, ROWS),
        old_list.reshape(1, ROWS),
        new_list.reshape(1, ROWS),
        pq_codes,
        centroids,
    )


def solution(mesh):
    return jax.shard_map(
        body,
        mesh=mesh,
        in_specs=(
            P(("lists", "rep"), None),
            P(("lists", "rep")),
            P(("lists", "rep")),
            P(("lists", "rep")),
            P(("lists", "rep"), None),
            P("lists", None),
        ),
        out_specs=(P("lists", "rep"), P("rep", None)),
        check_vma=False,
    )
```

time: 692 us -> 70.7 us (0.10)
  blocking collectives: 491 us -> 0 us
  Pallas kernels: 0 us -> 65.3 us
  local copies, waits for them, and re-layouts: 57.8 us -> 4.45 us
  waiting for transfers between devices: 52.6 us -> 0 us
  starting transfers between devices: 40.6 us -> 0 us
  matrix products: 16.6 us -> 0 us
  between operations: 14.7 us -> 0.7 us
  other arithmetic: 13 us -> 0 us
    psum x1 -> x0, blocking collectives: 491 us -> none  [body(): codebook = lax.psum(codebook, 'lists')]
    pallas_call x0 -> x1, Pallas kernels: none -> 65.3 us  [body(): pl.pallas_call(kernel, name='rebuild_window', out_shape=(jax.ShapeDtypeSt...]
    all_to_all x4 -> x0, starting transfers between devices: 40.5 us -> none  [the longest x1 18.4 us: body(): lax.all_to_all(send_scales, 'lists', split_axis=0, concat_axis=0, tiled=T...]
    all_to_all x4 -> x0, waiting for transfers between devices: 36 us -> none  [the longest x1 11.2 us: body(): lax.all_to_all(send_pq, 'lists', split_axis=0, concat_axis=0, tiled=True)]
    gather x14 -> x0, local copies, waits for them, and re-layouts: 17.8 us -> none  [the longest x8 10.7 us: body(): group_total.reshape(group_size, KSUB, group_size, sub_width)]
    dot_general x10 -> x0, matrix products: 16.6 us -> none  [the longest x8 14.4 us: body(): lax.dot_general(code_hits, columns, (((0,), (0,)), ((), ())), preferred_e...]
    reduce_scatter x2 -> x0, waiting for transfers between devices: 16.6 us -> none  [the longest x1 16.6 us: body(): lax.psum_scatter(codebook_part.astype(jnp.bfloat16), 'rep', scatter_dimen...]
    reshape x9 -> x0, local copies, waits for them, and re-layouts: 15.7 us -> none  [the longest x8 14.5 us: body(): results.append(diagonal.reshape(group_size, KSUB * sub_width))]
  transfers between devices with their start and end apart: 6 -> 0, of which waited for: 5 -> 0; matrix products, arithmetic and copies ran while one was open for 3% -> 0% of each run, Pallas kernels for 0% -> 0%
where the time goes in v1:
time: 70.7 us; the launch traced here: 70.4 us
  Pallas kernels  65.3 us (92%)
  local copies, waits for them, and re-layouts  4.45 us (6%)
    pallas_call x1, Pallas kernels, body(): pl.pallas_call(kernel, name='rebuild_window', out_shape=(jax.ShapeDtypeSt...  65.3 us
    unnamed x13, local copies, waits for them, and re-layouts  4.45 us

profile of v1, /device:TPU:1, one launch (start us, length us, event | category | flops | bytes accessed | tf_op | source)
XLA Modules:
  0.0 70.4 jit_solution(11861032645069511340)
XLA Ops:
  0.6 0.0 copy-start.2
  0.6 0.0 copy-start.3
  0.7 0.0 copy-start.4
  0.7 0.9 %copy.8.pq_ref = s32[128,64]{1,0:T(8,128)S(1)} copy(s32[128,64]{0,1:T(8,128)} %param.10) | data formatting | bytes 65536 | tf_op args[4]
  1.5 0.0 copy-done.2
  1.5 0.0 copy-done.3
  1.6 0.0 copy-done.4
  1.6 0.0 copy-start
  1.6 1.2 %copy-done = bf16[512,1024]{1,0:T(8,128)(2,1)S(1)} copy-done((bf16[512,1024]{1,0:T(8,128)(2,1)S(1)}, bf16[512,1024]{1,0:T(8,128)(2,1)}, u32[]{:S(2)}) %copy-start) | copy-done | bytes 1048600
  2.8 0.0 copy-start.1
  2.8 0.9 %copy-done.1 = bf16[128,1024]{1,0:T(8,128)(2,1)S(1)} copy-done((bf16[128,1024]{1,0:T(8,128)(2,1)S(1)}, bf16[128,1024]{1,0:T(8,128)(2,1)}, u32[]{:S(2)}) %copy-start.1) | copy-done | bytes 262168
  3.7 65.3 %rebuild_window.1 = (bf16[512,256]{1,0:T(8,128)(2,1)S(1)}, f32[16,4096]{1,0:T(8,128)S(1)}) custom-call(bf16[128,1024]{1,0:T(8,128)(2,1)S(1)} %copy-done.1, bf16[1,128]{1,0:T(2,128)(2,1)S(1)} %bitcast.3, s32[1,128]{1,0:T(1,128)S(1)} %bitcast.4, s32[1,128]{1,0:T(1,128)S(1)} %bitcast.5, s32[128,64]{1,0:T(8,128)S(1)} %copy.8.pq_ref, bf16[512,1024]{1,0:T(8,128)(2,1)S(1)} %copy-done), custom_call_target="tpu_custom_call" | custom-call | tf_op jit(solution)/shard_map/rebuild_window/pallas_call | solution.py:362
  69.0 0.7 %copy.11 = bf16[512,256]{1,0:T(8,128)(2,1)} copy(bf16[512,256]{1,0:T(8,128)(2,1)S(1)} %get-tuple-element.4) | data formatting | bytes 524288
  69.7 0.7 copy.12
Async XLA Ops:
  0.6 0.9 %copy-start.2 = (bf16[128]{0:T(256)(128)(2,1)S(1)}, bf16[128]{0:T(256)(128)(2,1)}, u32[]{:S(2)}) copy-start(bf16[128]{0:T(256)(128)(2,1)} %param.7) | copy-start | bytes 772
  0.6 0.9 %copy-start.3 = (s32[128]{0:T(128)S(1)}, s32[128]{0:T(128)}, u32[]{:S(2)}) copy-start(s32[128]{0:T(128)} %param.8) | copy-start | bytes 1540
  0.7 0.9 %copy-start.4 = (s32[128]{0:T(128)S(1)}, s32[128]{0:T(128)}, u32[]{:S(2)}) copy-start(s32[128]{0:T(128)} %param.9) | copy-start | bytes 1540
  1.6 1.2 %copy-start = (bf16[512,1024]{1,0:T(8,128)(2,1)S(1)}, bf16[512,1024]{1,0:T(8,128)(2,1)}, u32[]{:S(2)}) copy-start(bf16[512,1024]{1,0:T(8,128)(2,1)} %cent_hbm.1) | copy-start | bytes 3145732
  2.8 0.9 %copy-start.1 = (bf16[128,1024]{1,0:T(8,128)(2,1)S(1)}, bf16[128,1024]{1,0:T(8,128)(2,1)}, u32[]{:S(2)}) copy-start(bf16[128,1024]{1,0:T(8,128)(2,1)} %codes.1) | copy-start | bytes 786436

commit v2 on v1

--- a/solution.py
+++ b/solution.py
@@ -22,6 +22,7 @@
 SLOTS = 8
 KK = 16
 KSUB = 256
+UNROLL = 4
 NT = (((1,), (1,)), ((), ()))
 NN = (((1,), (0,)), ((), ()))
 
@@ -34,30 +35,60 @@
     return lax.broadcasted_iota(I32, shape, axis)
 
 
-def chip_at(chip, step):
-    off = lax.rem(step * 27, CHIPS)
-    y = lax.rem(chip // 8 + off // 8, 8)
-    z = lax.rem(lax.rem(chip, 8) + lax.rem(off, 8), 8)
-    return y * 8 + z
-
-
-def list_peer(me, step):
-    off = lax.rem(step * 53, N_LISTS)
-    y = lax.rem(me // 16 + off // 16, 8)
-    z = lax.rem(lax.rem(me // 2, 8) + lax.rem(off // 2, 8), 8)
-    c = lax.rem(lax.rem(me, 2) + lax.rem(off, 2), 2)
-    return (y * 8 + z) * 2 + c
+def wrap(value, size):
+    return jnp.where(value >= size, value - size, value)
+
+
+def each_peer(me, visit):
+    y, z, core = me // 16 * 16, lax.rem(me // 2, 8), lax.rem(me, 2)
+    places = [2 * wrap(z + i // 2, 8) + wrap(core + i % 2, 2) for i in range(16)]
+
+    def step(t, carry):
+        start = wrap(y + 16 * t, N_LISTS)
+        for i in range(16):
+            peer = wrap(start + 16 * (3 * (i // 2) % 8), N_LISTS) + places[i]
+            if i == 0:
+
+                @pl.when(t > 0)
+                def _():
+                    visit(peer)
+            else:
+                visit(peer)
+        return carry
+
+    lax.fori_loop(0, 8, step, 0)
+
+
+def each_chip(chip, visit):
+    y, z = chip // 8 * 8, lax.rem(chip, 8)
+    places = [wrap(z + i, 8) for i in range(8)]
+
+    def step(t, carry):
+        start = wrap(y + 8 * t, CHIPS)
+        for i in range(8):
+            there = wrap(start + 8 * (3 * i % 8), CHIPS) + places[i]
+            if i == 0:
+
+                @pl.when(t > 0)
+                def _():
+                    visit(there)
+            else:
+                visit(there)
+        return carry
+
+    lax.fori_loop(0, 8, step, 0)
 
 
 def kernel(
-    codes,
+    codes_hbm,
     scale_ref,
     old_ref,
     new_ref,
-    pq_ref,
+    pq_hbm,
     cent_hbm,
     delta_out,
     book_out,
+    pq,
     cent,
     xbuf,
     msend,
@@ -76,6 +107,7 @@
     rsbuf,
     tile,
     gathered,
+    pq_sem,
     cent_sem,
     loc_sem,
     xs_sem,
@@ -106,6 +138,8 @@
             src, dst, ssem, rsem, device_id=device, device_id_type=MESH
         )
 
+    pq_copy = pltpu.make_async_copy(pq_hbm, pq, pq_sem)
+    pq_copy.start()
     cent_copy = pltpu.make_async_copy(
         cent_hbm.at[:, pl.ds(pl.multiple_of(rep * COLS, COLS), COLS)], cent, cent_sem
     )
@@ -117,13 +151,10 @@
             barrier, inc=1, device_id={"rep": lax.rem(rep + k, N_REP)}, device_id_type=MESH
         )
 
-    def greet(k, carry):
-        pl.semaphore_signal(
-            barrier, inc=1, device_id={"lists": list_peer(me, k)}, device_id_type=MESH
-        )
-        return carry
-
-    lax.fori_loop(1, N_LISTS, greet, 0)
+    def greet(peer):
+        pl.semaphore_signal(barrier, inc=1, device_id={"lists": peer}, device_id_type=MESH)
+
+    each_peer(me, greet)
 
     scale = scale_ref[...].astype(F32)
     new = new_ref[...]
@@ -142,7 +173,8 @@
     pick = (line // 32) * 16 + 2 * lax.rem(line, 16) + lax.rem(line, 32) // 16
     pick = jnp.where(lax.rem(line, 16) < 8, pick, -1)
     chooser = jnp.where(pick == iota(shape, 1), 1.0, 0.0).astype(BF16)
-    meta = dot(chooser, pq_ref[...].astype(F32).astype(BF16), NT)
+    pq_copy.wait()
+    meta = dot(chooser, pq[...].astype(F32).astype(BF16))
     line = lax.rem(iota((N_REP * 32, ROWS), 0), 32)
     extra = (
         (8, (new_in - new_hi * 256).astype(F32)),
@@ -164,14 +196,14 @@
     for k in range(1, N_REP):
         peer = lax.rem(rep + k, N_REP)
         copy_to(
-            codes.at[:, pl.ds(pl.multiple_of(peer * COLS, COLS), COLS)],
+            codes_hbm.at[:, pl.ds(pl.multiple_of(peer * COLS, COLS), COLS)],
             xbuf.at[rep],
             xs_sem,
             xr_sem,
             rep=peer,
         ).start()
     own = pltpu.make_async_copy(
-        codes.at[:, pl.ds(pl.multiple_of(rep * COLS, COLS), COLS)], xbuf.at[rep], loc_sem
+        codes_hbm.at[:, pl.ds(pl.multiple_of(rep * COLS, COLS), COLS)], xbuf.at[rep], loc_sem
     )
     own.start()
     mrecv[rep] = msend[rep]
@@ -195,12 +227,10 @@
     )
     esend[...] = routed.reshape(N_LISTS, 1, SLOTS * KK)
 
-    def send_meta(k, carry):
-        peer = list_peer(me, k)
+    def send_meta(peer):
         copy_to(esend.at[peer], erecv.at[me], es_sem, er_sem, lists=peer).start()
-        return carry
-
-    lax.fori_loop(1, N_LISTS, send_meta, 0)
+
+    each_peer(me, send_meta)
     erecv[me] = esend[me]
 
     own.wait()
@@ -214,12 +244,10 @@
     moved = dot(move, x).reshape(N_LISTS, SLOTS, COLS)
     vsend[...] = jnp.concatenate([moved[:, :, 0:128], moved[:, :, 128:256]], axis=1).astype(BF16)
 
-    def send_vec(k, carry):
-        peer = list_peer(me, k)
+    def send_vec(peer):
         copy_to(vsend.at[peer], vrecv.at[me], vs_sem, vr_sem, lists=peer).start()
-        return carry
-
-    lax.fori_loop(1, N_LISTS, send_vec, 0)
+
+    each_peer(me, send_vec)
     vrecv[me] = vsend[me]
 
     scale = low[9:10, :]
@@ -228,21 +256,23 @@
     delta_acc[...] = dot(weight, x)
     pqk[0:8, 0:GROUP] = low[0:8, :]
     pqk[8:16, 0:GROUP] = high[0:8, :]
-    code = iota((KSUB, GROUP), 0).astype(F32)
     lane_sub = iota((KSUB, 128), 1) // 16
-
-    def value_sums(i, carry):
-        sub = 2 * lax.rem(i, 8) + i // 8
-        half = sub // 8
-        hits = jnp.where(code == pqk[pl.ds(i, 1), 0:GROUP], scale, 0.0).astype(BF16)
-        cols = xbuf[:, :, pl.ds(pl.multiple_of(half * 128, 128), 128)].reshape(GROUP, 128)
-        total = dot(hits, cols)
-        at = pl.ds(pl.multiple_of(half * KSUB, KSUB), KSUB)
-        book[at, :] = jnp.where(lane_sub == lax.rem(sub, 8), total, book[at, :])
-        return carry
-
-    book[...] = jnp.zeros_like(book)
-    lax.fori_loop(0, 16, value_sums, 0)
+    code = iota((KSUB, GROUP), 0).astype(F32).astype(BF16)
+    scale_b = jnp.broadcast_to(scale.astype(BF16), (KSUB, GROUP))
+    none = jnp.zeros((), BF16)
+    for half in range(2):
+        cols = x[:, half * 128 : (half + 1) * 128]
+
+        def value_sums(i, total):
+            row = (i // 4) * 8 + half * 4 + lax.rem(i, 4)
+            picks = pqk[pl.ds(row, 1), 0:GROUP].astype(BF16)
+            hits = jnp.where(code == picks, scale_b, none)
+            sub = 2 * lax.rem(i, 4) + i // 4
+            return jnp.where(lane_sub == sub, dot(hits, cols), total)
+
+        book[half * KSUB : (half + 1) * KSUB, :] = lax.fori_loop(
+            0, 8, value_sums, jnp.zeros((KSUB, 128), F32), unroll=UNROLL
+        )
 
     cent_copy.wait()
     eye = jnp.where(iota((COLS, COLS), 0) == iota((COLS, COLS), 1), 1.0, 0.0).astype(BF16)
@@ -266,24 +296,27 @@
     new_scale = jnp.concatenate(scale_rows, axis=1)
     inside = iota((LISTS, N_LISTS * SLOTS), 0).astype(F32) == new_in
     centg[...] = dot(cent_t, jnp.where(inside, 1.0, 0.0).astype(BF16)).astype(BF16)
-    code = iota((KSUB, N_LISTS * SLOTS), 0).astype(F32)
-
-    def cent_sums(i, carry):
-        sub = 2 * lax.rem(i, 8) + i // 8
-        half = sub // 8
-        hits = jnp.where(code == pqk[pl.ds(i, 1), :], 1.0, 0.0).astype(BF16)
-        total = dot(hits, centg[pl.ds(pl.multiple_of(half * 128, 128), 128), :], NT)
-        at = pl.ds(pl.multiple_of(half * KSUB, KSUB), KSUB)
-        book[at, :] = book[at, :] - jnp.where(lane_sub == lax.rem(sub, 8), total, 0.0)
-        return carry
-
-    lax.fori_loop(0, 16, cent_sums, 0)
-    comb[...] = book[...].reshape(CHIPS // 2, 2, 8, 128)
-
-    pair = copy_to(comb.at[:, 1 - core], sib, bs_sem, br_sem, lists=sibling)
-    pair.start()
-    pair.wait()
-    sib[...] = sib[...] + comb[:, core]
+    code = iota((KSUB, N_LISTS * SLOTS), 0).astype(F32).astype(BF16)
+    one = jnp.ones((), BF16)
+    pairs = []
+    for half in range(2):
+        cols = centg[half * 128 : (half + 1) * 128, :]
+
+        def cent_sums(i, total):
+            row = (i // 4) * 8 + half * 4 + lax.rem(i, 4)
+            picks = pqk[pl.ds(row, 1), :].astype(BF16)
+            hits = jnp.where(code == picks, one, none)
+            sub = 2 * lax.rem(i, 4) + i // 4
+            return jnp.where(lane_sub == sub, dot(hits, cols, NT), total)
+
+        total = lax.fori_loop(0, 8, cent_sums, jnp.zeros((KSUB, 128), F32), unroll=UNROLL)
+        part = pl.ds(half * 16, 16)
+        comb[part] = (book[half * KSUB : (half + 1) * KSUB, :] - total).reshape(16, 2, 8, 128)
+        pair = copy_to(
+            comb.at[part, 1 - core], sib.at[part], bs_sem.at[half], br_sem.at[half], lists=sibling
+        )
+        pair.start()
+        pairs.append(pair)
 
     def send_tile(q, carry):
         there = 2 * q + core
@@ -296,7 +329,11 @@
 
         return carry
 
-    lax.fori_loop(0, CHIPS // 2, send_tile, 0)
+    for half in range(2):
+        part = pl.ds(half * 16, 16)
+        pairs[half].wait()
+        sib[part] = sib[part] + comb[part, core]
+        lax.fori_loop(half * 16, half * 16 + 16, send_tile, 0)
     sums_here = lax.rem(chip, 2) == core
 
     @pl.when(sums_here)
@@ -311,24 +348,14 @@
             moved = pltpu.roll(pltpu.roll(total, 8 - d, 0), 16 * d, 1)
             turned = jnp.where(shift == d, moved, turned)
         tile[...] = turned
-        give = copy_to(tile, tile, ts_sem, tr_sem, lists=sibling)
-        give.start()
-        give.wait_send()
-        most = sib.at[pl.ds(0, CHIPS // 2 - 1)]
-        copy_to(most, most, rs_sem, rr_sem, lists=sibling).wait_send()
-
-    @pl.when(jnp.logical_not(sums_here))
-    def _():
-        copy_to(tile, tile, ts_sem, tr_sem, lists=sibling).wait_recv()
-        copy_to(sib, sib, rs_sem, rr_sem, lists=sibling).wait_send()
-
-    def send_sum(k, carry):
-        there = chip_at(chip, k)
-        copy_to(tile, gathered.at[chip], gs_sem, gr_sem, lists=2 * there + core).start()
-        return carry
-
-    lax.fori_loop(1, CHIPS, send_sum, 0)
-    gathered[chip] = tile[...]
+        gathered[core, chip // 2] = turned
+
+        def send_sum(there):
+            copy_to(
+                tile, gathered.at[core, chip // 2], gs_sem, gr_sem, lists=2 * there + core
+            ).start()
+
+        each_chip(chip, send_sum)
 
     most = vrecv.at[pl.ds(0, N_LISTS - 1)]
     wait = copy_to(most, most, vs_sem, vr_sem, lists=sibling)
@@ -348,17 +375,41 @@
     weight = jnp.where(inside, new_scale, 0.0).astype(BF16)
     delta_out[...] = (dot(weight, vecs) - delta_acc[...]).astype(BF16)
 
-    most = gathered.at[pl.ds(0, CHIPS - 1)]
-    wait = copy_to(most, most, gs_sem, gr_sem, lists=sibling)
-    wait.wait_recv()
-    wait.wait_send()
+    @pl.when(sums_here)
+    def _():
+        most = gathered.at[core, pl.ds(0, CHIPS // 2 - 1)]
+        copy_to(most, most, gs_sem, gr_sem, lists=sibling).wait_recv()
+
+    @pl.when(jnp.logical_not(sums_here))
+    def _():
+        most = gathered.at[core]
+        copy_to(most, most, gs_sem, gr_sem, lists=sibling).wait_recv()
+
+    give = copy_to(gathered.at[core], gathered.at[core], ts_sem, tr_sem, lists=sibling)
+    give.start()
+
+    @pl.when(sums_here)
+    def _():
+        most = rsbuf.at[pl.ds(0, CHIPS - 1)]
+        copy_to(most, most, gs_sem, gr_sem, lists=sibling).wait_send()
+        most = sib.at[pl.ds(0, CHIPS // 2 - 1)]
+        copy_to(most, most, rs_sem, rr_sem, lists=sibling).wait_send()
+
+    @pl.when(jnp.logical_not(sums_here))
+    def _():
+        copy_to(sib, sib, rs_sem, rr_sem, lists=sibling).wait_send()
+
+    give.wait()
     for t in range(CHIPS):
         half, block = t // 32, t % 32
-        book_out[half * 8 : half * 8 + 8, block * 128 : (block + 1) * 128] = gathered[t]
+        book_out[half * 8 : half * 8 + 8, block * 128 : (block + 1) * 128] = gathered[
+            t % 2, t // 2
+        ]
 
 
 def body(vector_codes, row_scales, old_list, new_list, pq_codes, centroids):
     vmem = pl.BlockSpec(memory_space=pltpu.VMEM)
+    hbm = pl.BlockSpec(memory_space=pltpu.HBM)
     return pl.pallas_call(
         kernel,
         name="rebuild_window",
@@ -366,9 +417,10 @@
             jax.ShapeDtypeStruct((LISTS, COLS), BF16),
             jax.ShapeDtypeStruct((16, 4096), F32),
         ),
-        in_specs=[vmem] * 5 + [pl.BlockSpec(memory_space=pl.ANY)],
+        in_specs=[hbm] + [vmem] * 3 + [hbm] * 2,
         out_specs=(vmem, vmem),
         scratch_shapes=[
+            pltpu.VMEM((64, ROWS), I32),
             pltpu.VMEM((LISTS, COLS), BF16),
             pltpu.VMEM((N_REP, ROWS, COLS), BF16),
             pltpu.VMEM((N_REP, 32, ROWS), BF16),
@@ -386,18 +438,20 @@
             pltpu.VMEM((CHIPS // 2, 2, 8, 128), F32),
             pltpu.VMEM((CHIPS, 8, 128), F32),
             pltpu.VMEM((8, 128), F32),
-            pltpu.VMEM((CHIPS, 8, 128), F32),
+            pltpu.VMEM((2, CHIPS // 2, 8, 128), F32),
         ]
-        + [pltpu.SemaphoreType.DMA] * 18,
+        + [pltpu.SemaphoreType.DMA] * 11
+        + [pltpu.SemaphoreType.DMA((2,))] * 2
+        + [pltpu.SemaphoreType.DMA] * 6,
         compiler_params=pltpu.CompilerParams(
-            collective_id=0, has_side_effects=True, vmem_limit_bytes=48 * 1024 * 1024
+            collective_id=0, has_side_effects=True, vmem_limit_bytes=56 * 1024 * 1024
         ),
     )(
         vector_codes,
         row_scales.reshape(1, ROWS),
         old_list.reshape(1, ROWS),
         new_list.reshape(1, ROWS),
-        pq_codes,
+        pq_codes.T,
         centroids,
     )
 

time: 70.7 us -> 58.6 us (0.83)
  Pallas kernels: 65.3 us -> 55.4 us
  local copies, waits for them, and re-layouts: 4.45 us -> 2.42 us
    pallas_call x1, Pallas kernels: 65.3 us -> 55.4 us  [body(): pl.pallas_call(kernel, name='rebuild_window', out_shape=(jax.ShapeDtypeSt...]
    unnamed x13 -> x4, local copies, waits for them, and re-layouts: 4.45 us -> 2.42 us
where the time goes in v2:
time: 58.6 us; the launch traced here: 58.5 us
  Pallas kernels  55.4 us (95%)
  local copies, waits for them, and re-layouts  2.42 us (4%)
  between operations  0.65 us (1%)
    pallas_call x1, Pallas kernels, body(): pl.pallas_call(kernel, name='rebuild_window', out_shape=(jax.ShapeDtypeSt...  55.4 us
    unnamed x4, local copies, waits for them, and re-layouts  2.42 us

profile of v2, /device:TPU:1, one launch (start us, length us, event | category | flops | bytes accessed | tf_op | source)
XLA Modules:
  0.0 58.5 jit_solution(14078371447724601522)
XLA Ops:
  0.6 55.4 %rebuild_window.1 = (bf16[512,256]{1,0:T(8,128)(2,1)}, f32[16,4096]{1,0:T(8,128)}) custom-call(bf16[128,1024]{1,0:T(8,128)(2,1)} %codes_hbm.1, bf16[1,128]{1,0:T(2,128)(2,1)} %bitcast.5, s32[1,128]{1,0:T(1,128)} %bitcast.6, s32[1,128]{1,0:T(1,128)} %bitcast.7, s32[64,128]{1,0:T(8,128)} %bitcast.4, bf16[512,1024]{1,0:T(8,128)(2,1)} %cent_hbm.1), custom_call_target="tpu_custom_call" | custom-call | tf_op jit(solution)/shard_map/rebuild_window/pallas_call | solution.py:413
  56.0 0.0 copy-start
  56.1 1.7 %copy.10 = bf16[512,256]{1,0:T(8,128)(2,1)} copy(bf16[512,256]{1,0:T(8,128)(2,1)} %get-tuple-element.4) | data formatting | bytes 524288
  57.8 0.0 copy-done
  57.8 0.7 %copy.11 = f32[16,4096]{1,0:T(8,128)} copy(f32[16,4096]{1,0:T(8,128)S(1)} %copy-done) | data formatting | bytes 524288
Async XLA Ops:
  56.0 1.7 %copy-start = (f32[16,4096]{1,0:T(8,128)S(1)}, f32[16,4096]{1,0:T(8,128)}, u32[]{:S(2)}) copy-start(f32[16,4096]{1,0:T(8,128)} %get-tuple-element.5) | copy-start | bytes 786436

commit v3 on v2

--- a/solution.py
+++ b/solution.py
@@ -22,7 +22,8 @@
 SLOTS = 8
 KK = 16
 KSUB = 256
-UNROLL = 4
+STACK = 4
+V1, V2, V3 = 4, 6, 8
 NT = (((1,), (1,)), ((), ()))
 NN = (((1,), (0,)), ((), ()))
 
@@ -39,7 +40,7 @@
     return jnp.where(value >= size, value - size, value)
 
 
-def each_peer(me, visit):
+def each_peer(me, visit, first=0, last=8):
     y, z, core = me // 16 * 16, lax.rem(me // 2, 8), lax.rem(me, 2)
     places = [2 * wrap(z + i // 2, 8) + wrap(core + i % 2, 2) for i in range(16)]
 
@@ -56,7 +57,7 @@
                 visit(peer)
         return carry
 
-    lax.fori_loop(0, 8, step, 0)
+    lax.fori_loop(first, last, step, 0)
 
 
 def each_chip(chip, visit):
@@ -81,13 +82,16 @@
 
 def kernel(
     codes_hbm,
-    scale_ref,
-    old_ref,
-    new_ref,
+    scale_hbm,
+    old_hbm,
+    new_hbm,
     pq_hbm,
     cent_hbm,
     delta_out,
     book_out,
+    scale_ref,
+    old_ref,
+    new_ref,
     pq,
     cent,
     xbuf,
@@ -107,6 +111,7 @@
     rsbuf,
     tile,
     gathered,
+    in_sem,
     pq_sem,
     cent_sem,
     loc_sem,
@@ -126,6 +131,7 @@
     tr_sem,
     gs_sem,
     gr_sem,
+    row_sem,
 ):
     me = lax.axis_index("lists")
     rep = lax.axis_index("rep")
@@ -138,6 +144,14 @@
             src, dst, ssem, rsem, device_id=device, device_id_type=MESH
         )
 
+    small_copies = [
+        pltpu.make_async_copy(src, dst, in_sem.at[i])
+        for i, (src, dst) in enumerate(
+            ((new_hbm, new_ref), (old_hbm, old_ref), (scale_hbm, scale_ref))
+        )
+    ]
+    for small in small_copies:
+        small.start()
     pq_copy = pltpu.make_async_copy(pq_hbm, pq, pq_sem)
     pq_copy.start()
     cent_copy = pltpu.make_async_copy(
@@ -151,11 +165,15 @@
             barrier, inc=1, device_id={"rep": lax.rem(rep + k, N_REP)}, device_id_type=MESH
         )
 
-    def greet(peer):
-        pl.semaphore_signal(barrier, inc=1, device_id={"lists": peer}, device_id_type=MESH)
-
-    each_peer(me, greet)
-
+    for k in range(1, 16):
+        row_peer = me // 16 * 16 + lax.rem(me + k, 16)
+        pl.semaphore_signal(barrier, inc=1, device_id={"lists": row_peer}, device_id_type=MESH)
+    for k in range(1, 8):
+        column_peer = lax.rem(me + 16 * k, N_LISTS)
+        pl.semaphore_signal(barrier, inc=1, device_id={"lists": column_peer}, device_id_type=MESH)
+
+    for small in small_copies:
+        small.wait()
     scale = scale_ref[...].astype(F32)
     new = new_ref[...]
     owner = new // LISTS
@@ -188,7 +206,10 @@
         meta = jnp.where(line == at, row, meta)
     msend[...] = meta.astype(BF16).reshape(N_REP, 32, ROWS)
 
-    pl.semaphore_wait(barrier, N_LISTS - 1 + N_REP - 1)
+    pl.semaphore_wait(barrier, N_REP - 1 + 15 + 7)
+    for k in range(1, 8):
+        column_peer = lax.rem(me + 16 * k, N_LISTS)
+        pl.semaphore_signal(row_sem, inc=1, device_id={"lists": column_peer}, device_id_type=MESH)
 
     for k in range(1, N_REP):
         peer = lax.rem(rep + k, N_REP)
@@ -230,6 +251,7 @@
     def send_meta(peer):
         copy_to(esend.at[peer], erecv.at[me], es_sem, er_sem, lists=peer).start()
 
+    pl.semaphore_wait(row_sem, 7)
     each_peer(me, send_meta)
     erecv[me] = esend[me]
 
@@ -247,7 +269,7 @@
     def send_vec(peer):
         copy_to(vsend.at[peer], vrecv.at[me], vs_sem, vr_sem, lists=peer).start()
 
-    each_peer(me, send_vec)
+    each_peer(me, send_vec, 0, V1)
     vrecv[me] = vsend[me]
 
     scale = low[9:10, :]
@@ -260,19 +282,25 @@
     code = iota((KSUB, GROUP), 0).astype(F32).astype(BF16)
     scale_b = jnp.broadcast_to(scale.astype(BF16), (KSUB, GROUP))
     none = jnp.zeros((), BF16)
+
+    def code_sums(hits_of, half, cols, dims):
+        total = jnp.zeros((KSUB, 128), F32)
+        for first in range(0, 8, STACK):
+            these = range(first, first + STACK)
+            hits = [hits_of((i // 4) * 8 + half * 4 + i % 4) for i in these]
+            sums = dot(jnp.concatenate(hits, axis=0), cols, dims)
+            for at, i in enumerate(these):
+                own = lane_sub == 2 * (i % 4) + i // 4
+                total = jnp.where(own, sums[at * KSUB : (at + 1) * KSUB, :], total)
+        return total
+
     for half in range(2):
         cols = x[:, half * 128 : (half + 1) * 128]
 
-        def value_sums(i, total):
-            row = (i // 4) * 8 + half * 4 + lax.rem(i, 4)
-            picks = pqk[pl.ds(row, 1), 0:GROUP].astype(BF16)
-            hits = jnp.where(code == picks, scale_b, none)
-            sub = 2 * lax.rem(i, 4) + i // 4
-            return jnp.where(lane_sub == sub, dot(hits, cols), total)
-
-        book[half * KSUB : (half + 1) * KSUB, :] = lax.fori_loop(
-            0, 8, value_sums, jnp.zeros((KSUB, 128), F32), unroll=UNROLL
-        )
+        def value_hits(row):
+            return jnp.where(code == pqk[row : row + 1, 0:GROUP].astype(BF16), scale_b, none)
+
+        book[half * KSUB : (half + 1) * KSUB, :] = code_sums(value_hits, half, cols, NN)
 
     cent_copy.wait()
     eye = jnp.where(iota((COLS, COLS), 0) == iota((COLS, COLS), 1), 1.0, 0.0).astype(BF16)
@@ -282,6 +310,7 @@
     wait = copy_to(most, most, es_sem, er_sem, lists=sibling)
     wait.wait_recv()
     wait.wait_send()
+    each_peer(me, send_vec, V1, V2)
     got = jnp.transpose(erecv[...].reshape(N_LISTS, SLOTS * KK))
     new_rows = []
     scale_rows = []
@@ -302,14 +331,10 @@
     for half in range(2):
         cols = centg[half * 128 : (half + 1) * 128, :]
 
-        def cent_sums(i, total):
-            row = (i // 4) * 8 + half * 4 + lax.rem(i, 4)
-            picks = pqk[pl.ds(row, 1), :].astype(BF16)
-            hits = jnp.where(code == picks, one, none)
-            sub = 2 * lax.rem(i, 4) + i // 4
-            return jnp.where(lane_sub == sub, dot(hits, cols, NT), total)
-
-        total = lax.fori_loop(0, 8, cent_sums, jnp.zeros((KSUB, 128), F32), unroll=UNROLL)
+        def cent_hits(row):
+            return jnp.where(code == pqk[row : row + 1, :].astype(BF16), one, none)
+
+        total = code_sums(cent_hits, half, cols, NT)
         part = pl.ds(half * 16, 16)
         comb[part] = (book[half * KSUB : (half + 1) * KSUB, :] - total).reshape(16, 2, 8, 128)
         pair = copy_to(
@@ -318,27 +343,43 @@
         pair.start()
         pairs.append(pair)
 
-    def send_tile(q, carry):
-        there = 2 * q + core
-
-        @pl.when(there != chip)
-        def _():
-            copy_to(
-                sib.at[q], rsbuf.at[chip], rs_sem, rr_sem, lists=2 * there + core
-            ).start()
-
-        return carry
+    y, z = chip // 8, lax.rem(chip, 8)
+    block = z // 4
+
+    def send_tiles(half):
+        def step(t, carry):
+            row = wrap(y + t, 8)
+            odd = lax.rem(row + half, 2)
+            for i in range(2):
+                col = wrap(block + i, 2)
+                there = row * 8 + 4 * col + 2 * odd + core
+
+                @pl.when(there != chip)
+                def _():
+                    copy_to(
+                        sib.at[half * 16 + row * 2 + col],
+                        rsbuf.at[chip],
+                        rs_sem,
+                        rr_sem,
+                        lists=2 * there + core,
+                    ).start()
+
+            return carry
+
+        lax.fori_loop(0, 8, step, 0)
 
     for half in range(2):
         part = pl.ds(half * 16, 16)
         pairs[half].wait()
         sib[part] = sib[part] + comb[part, core]
-        lax.fori_loop(half * 16, half * 16 + 16, send_tile, 0)
-    sums_here = lax.rem(chip, 2) == core
+        send_tiles(half)
+    each_peer(me, send_vec, V2, V3)
+    mine = lax.rem(y + z // 2, 2) * 16 + y * 2 + block
+    sums_here = lax.rem(z, 2) == core
 
     @pl.when(sums_here)
     def _():
-        rsbuf[chip] = sib[chip // 2]
+        rsbuf[chip] = sib[mine]
         most = rsbuf.at[pl.ds(0, CHIPS - 1)]
         copy_to(most, most, rs_sem, rr_sem, lists=sibling).wait_recv()
         total = jnp.sum(rsbuf[...], axis=0)
@@ -348,14 +389,16 @@
             moved = pltpu.roll(pltpu.roll(total, 8 - d, 0), 16 * d, 1)
             turned = jnp.where(shift == d, moved, turned)
         tile[...] = turned
-        gathered[core, chip // 2] = turned
+        gathered[core, mine] = turned
 
         def send_sum(there):
             copy_to(
-                tile, gathered.at[core, chip // 2], gs_sem, gr_sem, lists=2 * there + core
+                tile, gathered.at[core, mine], gs_sem, gr_sem, lists=2 * there + core
             ).start()
 
         each_chip(chip, send_sum)
+
+    each_peer(me, send_vec, V3, 8)
 
     most = vrecv.at[pl.ds(0, N_LISTS - 1)]
     wait = copy_to(most, most, vs_sem, vr_sem, lists=sibling)
@@ -414,12 +457,15 @@
         kernel,
         name="rebuild_window",
         out_shape=(
-            jax.ShapeDtypeStruct((LISTS, COLS), BF16),
-            jax.ShapeDtypeStruct((16, 4096), F32),
+            pltpu.VMEM((LISTS, COLS), BF16),
+            pltpu.VMEM((16, 4096), F32),
         ),
-        in_specs=[hbm] + [vmem] * 3 + [hbm] * 2,
+        in_specs=[hbm] * 6,
         out_specs=(vmem, vmem),
         scratch_shapes=[
+            pltpu.VMEM((1, ROWS), BF16),
+            pltpu.VMEM((1, ROWS), I32),
+            pltpu.VMEM((1, ROWS), I32),
             pltpu.VMEM((64, ROWS), I32),
             pltpu.VMEM((LISTS, COLS), BF16),
             pltpu.VMEM((N_REP, ROWS, COLS), BF16),
@@ -440,9 +486,11 @@
             pltpu.VMEM((8, 128), F32),
             pltpu.VMEM((2, CHIPS // 2, 8, 128), F32),
         ]
+        + [pltpu.SemaphoreType.DMA((3,))]
         + [pltpu.SemaphoreType.DMA] * 11
         + [pltpu.SemaphoreType.DMA((2,))] * 2
-        + [pltpu.SemaphoreType.DMA] * 6,
+        + [pltpu.SemaphoreType.DMA] * 6
+        + [pltpu.SemaphoreType.REGULAR],
         compiler_params=pltpu.CompilerParams(
             collective_id=0, has_side_effects=True, vmem_limit_bytes=56 * 1024 * 1024
         ),

time: 58.6 us -> 51.5 us (0.88)
  Pallas kernels: 55.4 us -> 49.4 us
  local copies, waits for them, and re-layouts: 2.42 us -> 1.41 us
    pallas_call x1, Pallas kernels: 55.4 us -> 49.4 us  [body(): pl.pallas_call(kernel, name='rebuild_window', out_shape=(pltpu.VMEM((LIST...]
    unnamed x4 -> x2, local copies, waits for them, and re-layouts: 2.42 us -> 1.41 us
where the time goes in v3:
time: 51.5 us; the launch traced here: 51.4 us
  Pallas kernels  49.4 us (96%)
  local copies, waits for them, and re-layouts  1.41 us (3%)
  between operations  0.64 us (1%)
    pallas_call x1, Pallas kernels, body(): pl.pallas_call(kernel, name='rebuild_window', out_shape=(pltpu.VMEM((LIST...  49.4 us
    unnamed x2, local copies, waits for them, and re-layouts  1.41 us

profile of v3, /device:TPU:1, one launch (start us, length us, event | category | flops | bytes accessed | tf_op | source)
XLA Modules:
  0.0 51.4 jit_solution(2860180174204964251)
XLA Ops:
  0.6 49.4 %rebuild_window.1 = (bf16[512,256]{1,0:T(8,128)(2,1)S(1)}, f32[16,4096]{1,0:T(8,128)S(1)}) custom-call(bf16[128,1024]{1,0:T(8,128)(2,1)} %codes_hbm.1, bf16[1,128]{1,0:T(2,128)(2,1)} %bitcast.5, s32[1,128]{1,0:T(1,128)} %bitcast.6, s32[1,128]{1,0:T(1,128)} %bitcast.7, s32[64,128]{1,0:T(8,128)} %bitcast.4, bf16[512,1024]{1,0:T(8,128)(2,1)} %cent_hbm.1), custom_call_target="tpu_custom_call" | custom-call | tf_op jit(solution)/shard_map/rebuild_window/pallas_call | solution.py:456
  50.0 0.7 %copy.10 = bf16[512,256]{1,0:T(8,128)(2,1)} copy(bf16[512,256]{1,0:T(8,128)(2,1)S(1)} %get-tuple-element.2) | data formatting | bytes 524288
  50.7 0.7 %copy.11 = f32[16,4096]{1,0:T(8,128)} copy(f32[16,4096]{1,0:T(8,128)S(1)} %get-tuple-element.3) | data formatting | bytes 524288

commit v4 on v3

--- a/solution.py
+++ b/solution.py
@@ -60,24 +60,14 @@
     lax.fori_loop(first, last, step, 0)
 
 
-def each_chip(chip, visit):
-    y, z = chip // 8 * 8, lax.rem(chip, 8)
-    places = [wrap(z + i, 8) for i in range(8)]
-
-    def step(t, carry):
-        start = wrap(y + 8 * t, CHIPS)
-        for i in range(8):
-            there = wrap(start + 8 * (3 * i % 8), CHIPS) + places[i]
-            if i == 0:
-
-                @pl.when(t > 0)
-                def _():
-                    visit(there)
-            else:
-                visit(there)
-        return carry
-
-    lax.fori_loop(0, 8, step, 0)
+def hops(step):
+    return min(step, 8 - step)
+
+
+FAR_FIRST = sorted(
+    ((dy, dz) for dy in range(8) for dz in range(8)), key=lambda d: -hops(d[0]) - hops(d[1])
+)
+FAR_RING = sorted(range(1, 8), key=lambda d: -hops(d))
 
 
 def kernel(
@@ -160,17 +150,18 @@
     cent_copy.start()
 
     barrier = pltpu.get_barrier_semaphore()
-    for k in range(1, N_REP):
+    y, z = chip // 8, lax.rem(chip, 8)
+    rows = [16 * wrap(y + d, 8) for d in range(8)]
+    places = [2 * wrap(z + d, 8) for d in range(8)]
+    for k in (2, 1, 3):
         pl.semaphore_signal(
             barrier, inc=1, device_id={"rep": lax.rem(rep + k, N_REP)}, device_id_type=MESH
         )
 
-    for k in range(1, 16):
-        row_peer = me // 16 * 16 + lax.rem(me + k, 16)
-        pl.semaphore_signal(barrier, inc=1, device_id={"lists": row_peer}, device_id_type=MESH)
-    for k in range(1, 8):
-        column_peer = lax.rem(me + 16 * k, N_LISTS)
-        pl.semaphore_signal(barrier, inc=1, device_id={"lists": column_peer}, device_id_type=MESH)
+    for d in FAR_RING:
+        for peer in (rows[d] + places[0] + core, rows[0] + places[d], rows[0] + places[d] + 1):
+            pl.semaphore_signal(barrier, inc=1, device_id={"lists": peer}, device_id_type=MESH)
+    pl.semaphore_signal(barrier, inc=1, device_id={"lists": sibling}, device_id_type=MESH)
 
     for small in small_copies:
         small.wait()
@@ -207,14 +198,14 @@
     msend[...] = meta.astype(BF16).reshape(N_REP, 32, ROWS)
 
     pl.semaphore_wait(barrier, N_REP - 1 + 15 + 7)
-    for k in range(1, 8):
-        column_peer = lax.rem(me + 16 * k, N_LISTS)
+    for d in FAR_RING:
+        column_peer = rows[d] + places[0] + core
         pl.semaphore_signal(row_sem, inc=1, device_id={"lists": column_peer}, device_id_type=MESH)
 
-    for k in range(1, N_REP):
+    for k in (2, 1, 3):
         peer = lax.rem(rep + k, N_REP)
         copy_to(msend.at[peer], mrecv.at[rep], ms_sem, mr_sem, rep=peer).start()
-    for k in range(1, N_REP):
+    for k in (2, 1, 3):
         peer = lax.rem(rep + k, N_REP)
         copy_to(
             codes_hbm.at[:, pl.ds(pl.multiple_of(peer * COLS, COLS), COLS)],
@@ -252,7 +243,10 @@
         copy_to(esend.at[peer], erecv.at[me], es_sem, er_sem, lists=peer).start()
 
     pl.semaphore_wait(row_sem, 7)
-    each_peer(me, send_meta)
+    for dy, dz in FAR_FIRST[:-1]:
+        send_meta(rows[dy] + places[dz])
+        send_meta(rows[dy] + places[dz] + 1)
+    send_meta(sibling)
     erecv[me] = esend[me]
 
     own.wait()
@@ -343,30 +337,30 @@
         pair.start()
         pairs.append(pair)
 
-    y, z = chip // 8, lax.rem(chip, 8)
     block = z // 4
 
     def send_tiles(half):
-        def step(t, carry):
-            row = wrap(y + t, 8)
-            odd = lax.rem(row + half, 2)
-            for i in range(2):
-                col = wrap(block + i, 2)
-                there = row * 8 + 4 * col + 2 * odd + core
-
-                @pl.when(there != chip)
-                def _():
-                    copy_to(
-                        sib.at[half * 16 + row * 2 + col],
-                        rsbuf.at[chip],
-                        rs_sem,
-                        rr_sem,
-                        lists=2 * there + core,
-                    ).start()
-
-            return carry
-
-        lax.fori_loop(0, 8, step, 0)
+        def send_tile(dy, near):
+            row = wrap(y + dy, 8)
+            place = 2 * lax.rem(row + half, 2) + core
+            ahead = wrap(place - z + 8, 8)
+            close = (ahead <= 2) | (ahead >= 6)
+            col = jnp.where(close, 1 - near, near)
+            there = row * 8 + 4 * col + place
+
+            @pl.when(there != chip)
+            def _():
+                copy_to(
+                    sib.at[half * 16 + row * 2 + col],
+                    rsbuf.at[chip],
+                    rs_sem,
+                    rr_sem,
+                    lists=2 * there + core,
+                ).start()
+
+        far_first = [(dy, near) for dy in range(8) for near in range(2)]
+        for dy, near in sorted(far_first, key=lambda d: 2 * d[1] - hops(d[0])):
+            send_tile(dy, near)
 
     for half in range(2):
         part = pl.ds(half * 16, 16)
@@ -391,12 +385,13 @@
         tile[...] = turned
         gathered[core, mine] = turned
 
-        def send_sum(there):
+        def send_sum(peer):
             copy_to(
-                tile, gathered.at[core, mine], gs_sem, gr_sem, lists=2 * there + core
+                tile, gathered.at[core, mine], gs_sem, gr_sem, lists=peer
             ).start()
 
-        each_chip(chip, send_sum)
+        for dy, dz in FAR_FIRST[:-1]:
+            send_sum(rows[dy] + places[dz] + core)
 
     each_peer(me, send_vec, V3, 8)
 

time: 51.5 us -> 49.5 us (0.961)
  Pallas kernels: 49.4 us -> 47.4 us
    pallas_call x1, Pallas kernels: 49.4 us -> 47.4 us  [body(): pl.pallas_call(kernel, name='rebuild_window', out_shape=(pltpu.VMEM((LIST...]
where the time goes in v4:
time: 49.5 us; the launch traced here: 49.4 us
  Pallas kernels  47.4 us (96%)
  local copies, waits for them, and re-layouts  1.41 us (3%)
  between operations  0.64 us (1%)
    pallas_call x1, Pallas kernels, body(): pl.pallas_call(kernel, name='rebuild_window', out_shape=(pltpu.VMEM((LIST...  47.4 us
    unnamed x2, local copies, waits for them, and re-layouts  1.41 us

profile of v4, /device:TPU:1, one launch (start us, length us, event | category | flops | bytes accessed | tf_op | source)
XLA Modules:
  0.0 49.4 jit_solution(16890780993941073371)
XLA Ops:
  0.6 47.4 %rebuild_window.1 = (bf16[512,256]{1,0:T(8,128)(2,1)S(1)}, f32[16,4096]{1,0:T(8,128)S(1)}) custom-call(bf16[128,1024]{1,0:T(8,128)(2,1)} %codes_hbm.1, bf16[1,128]{1,0:T(2,128)(2,1)} %bitcast.5, s32[1,128]{1,0:T(1,128)} %bitcast.6, s32[1,128]{1,0:T(1,128)} %bitcast.7, s32[64,128]{1,0:T(8,128)} %bitcast.4, bf16[512,1024]{1,0:T(8,128)(2,1)} %cent_hbm.1), custom_call_target="tpu_custom_call" | custom-call | tf_op jit(solution)/shard_map/rebuild_window/pallas_call | solution.py:451
  48.0 0.7 %copy.10 = bf16[512,256]{1,0:T(8,128)(2,1)} copy(bf16[512,256]{1,0:T(8,128)(2,1)S(1)} %get-tuple-element.2) | data formatting | bytes 524288
  48.7 0.7 %copy.11 = f32[16,4096]{1,0:T(8,128)} copy(f32[16,4096]{1,0:T(8,128)S(1)} %get-tuple-element.3) | data formatting | bytes 524288

commit v5 on v4

--- a/solution.py
+++ b/solution.py
@@ -23,7 +23,7 @@
 KK = 16
 KSUB = 256
 STACK = 4
-V1, V2, V3 = 4, 6, 8
+V1, V2, V3 = 40, 40, 63
 NT = (((1,), (1,)), ((), ()))
 NN = (((1,), (0,)), ((), ()))
 
@@ -40,33 +40,16 @@
     return jnp.where(value >= size, value - size, value)
 
 
-def each_peer(me, visit, first=0, last=8):
-    y, z, core = me // 16 * 16, lax.rem(me // 2, 8), lax.rem(me, 2)
-    places = [2 * wrap(z + i // 2, 8) + wrap(core + i % 2, 2) for i in range(16)]
-
-    def step(t, carry):
-        start = wrap(y + 16 * t, N_LISTS)
-        for i in range(16):
-            peer = wrap(start + 16 * (3 * (i // 2) % 8), N_LISTS) + places[i]
-            if i == 0:
-
-                @pl.when(t > 0)
-                def _():
-                    visit(peer)
-            else:
-                visit(peer)
-        return carry
-
-    lax.fori_loop(first, last, step, 0)
-
-
 def hops(step):
     return min(step, 8 - step)
 
 
-FAR_FIRST = sorted(
-    ((dy, dz) for dy in range(8) for dz in range(8)), key=lambda d: -hops(d[0]) - hops(d[1])
+NEAR_FIRST = sorted(
+    ((dy, dz) for dy in range(8) for dz in range(8)), key=lambda d: hops(d[0]) + hops(d[1])
 )
+FAR_FIRST = NEAR_FIRST[:0:-1]
+SPREAD = [(k * 27 % CHIPS // 8, k * 27 % 8) for k in range(1, CHIPS)]
+HALF = N_LISTS // 2
 FAR_RING = sorted(range(1, 8), key=lambda d: -hops(d))
 
 
@@ -239,15 +222,22 @@
     )
     esend[...] = routed.reshape(N_LISTS, 1, SLOTS * KK)
 
-    def send_meta(peer):
-        copy_to(esend.at[peer], erecv.at[me], es_sem, er_sem, lists=peer).start()
+    def send_meta(peer, step):
+        place = NEAR_FIRST.index(step)
+        copy_to(
+            esend.at[peer],
+            erecv.at[2 * place + core],
+            es_sem,
+            er_sem.at[2 * place // HALF],
+            lists=peer,
+        ).start()
 
     pl.semaphore_wait(row_sem, 7)
-    for dy, dz in FAR_FIRST[:-1]:
-        send_meta(rows[dy] + places[dz])
-        send_meta(rows[dy] + places[dz] + 1)
-    send_meta(sibling)
-    erecv[me] = esend[me]
+    for dy, dz in FAR_FIRST:
+        send_meta(rows[dy] + places[dz], (dy, dz))
+        send_meta(rows[dy] + places[dz] + 1, (dy, dz))
+    send_meta(sibling, (0, 0))
+    erecv[core] = esend[me]
 
     own.wait()
     three = xbuf.at[pl.ds(0, N_REP - 1)]
@@ -260,11 +250,20 @@
     moved = dot(move, x).reshape(N_LISTS, SLOTS, COLS)
     vsend[...] = jnp.concatenate([moved[:, :, 0:128], moved[:, :, 128:256]], axis=1).astype(BF16)
 
-    def send_vec(peer):
-        copy_to(vsend.at[peer], vrecv.at[me], vs_sem, vr_sem, lists=peer).start()
-
-    each_peer(me, send_vec, 0, V1)
-    vrecv[me] = vsend[me]
+    def send_vec(peer, step):
+        place = NEAR_FIRST.index(step)
+        copy_to(
+            vsend.at[peer], vrecv.at[2 * place + core], vs_sem, vr_sem, lists=peer
+        ).start()
+
+    def send_vecs(first, last):
+        for dy, dz in SPREAD[first:last]:
+            send_vec(rows[dy] + places[dz], (dy, dz))
+            send_vec(rows[dy] + places[dz] + 1, (dy, dz))
+
+    send_vec(sibling, (0, 0))
+    send_vecs(0, V1)
+    vrecv[core] = vsend[me]
 
     scale = low[9:10, :]
     old_in = low[11:12, :] + 256.0 * high[11:12, :]
@@ -300,35 +299,49 @@
     eye = jnp.where(iota((COLS, COLS), 0) == iota((COLS, COLS), 1), 1.0, 0.0).astype(BF16)
     cent_t = dot(eye, cent[...], NT).astype(BF16)
 
-    most = erecv.at[pl.ds(0, N_LISTS - 1)]
-    wait = copy_to(most, most, es_sem, er_sem, lists=sibling)
-    wait.wait_recv()
-    wait.wait_send()
-    each_peer(me, send_vec, V1, V2)
-    got = jnp.transpose(erecv[...].reshape(N_LISTS, SLOTS * KK))
-    new_rows = []
-    scale_rows = []
-    for q in range(SLOTS):
-        pairs = got[q * KK : q * KK + 8, :]
-        odd = jnp.floor(pairs * (1.0 / 256.0))
-        pqk[0:8, q * 128 : (q + 1) * 128] = pairs - 256.0 * odd
-        pqk[8:16, q * 128 : (q + 1) * 128] = odd
-        new_rows.append(got[q * KK + 8 : q * KK + 9, :])
-        scale_rows.append(got[q * KK + 9 : q * KK + 10, :])
-    new_in = jnp.concatenate(new_rows, axis=1) - 1.0
-    new_scale = jnp.concatenate(scale_rows, axis=1)
-    inside = iota((LISTS, N_LISTS * SLOTS), 0).astype(F32) == new_in
-    centg[...] = dot(cent_t, jnp.where(inside, 1.0, 0.0).astype(BF16)).astype(BF16)
-    code = iota((KSUB, N_LISTS * SLOTS), 0).astype(F32).astype(BF16)
+    code = iota((KSUB, HALF * SLOTS), 0).astype(F32).astype(BF16)
     one = jnp.ones((), BF16)
+
+    def unpack(part):
+        held = erecv[part * HALF : (part + 1) * HALF].reshape(HALF, SLOTS * KK)
+        held = jnp.concatenate([held, pltpu.roll(held, SLOTS * KK - KK, 1)], axis=0)
+        got = jnp.transpose(held)
+        new_rows = []
+        scale_rows = []
+        for q in range(0, SLOTS, 2):
+            pairs = got[q * KK : q * KK + 8, :]
+            odd = jnp.floor(pairs * (1.0 / 256.0))
+            at = part * HALF * SLOTS + q * HALF
+            pqk[0:8, at : at + 128] = pairs - 256.0 * odd
+            pqk[8:16, at : at + 128] = odd
+            new_rows.append(got[q * KK + 8 : q * KK + 9, :])
+            scale_rows.append(got[q * KK + 9 : q * KK + 10, :])
+        new_in = jnp.concatenate(new_rows, axis=1) - 1.0
+        inside = iota((LISTS, HALF * SLOTS), 0).astype(F32) == new_in
+        centg[part] = dot(cent_t, jnp.where(inside, 1.0, 0.0).astype(BF16)).astype(BF16)
+        return inside, jnp.concatenate(scale_rows, axis=1)
+
+    def cent_sums(part, half):
+        lanes = slice(part * HALF * SLOTS, (part + 1) * HALF * SLOTS)
+
+        def cent_hits(row):
+            return jnp.where(code == pqk[row : row + 1, lanes].astype(BF16), one, none)
+
+        return code_sums(cent_hits, half, centg[part, half * 128 : (half + 1) * 128, :], NT)
+
+    most = erecv.at[pl.ds(0, HALF - 1)]
+    copy_to(most, most, es_sem, er_sem.at[0], lists=sibling).wait_recv()
+    near_inside, near_scale = unpack(0)
+    for half in range(2):
+        at = slice(half * KSUB, (half + 1) * KSUB)
+        book[at, :] = book[at, :] - cent_sums(0, half)
+    send_vecs(V1, V2)
+    most = erecv.at[pl.ds(HALF, HALF)]
+    copy_to(most, most, es_sem, er_sem.at[1], lists=sibling).wait_recv()
+    far_inside, far_scale = unpack(1)
     pairs = []
     for half in range(2):
-        cols = centg[half * 128 : (half + 1) * 128, :]
-
-        def cent_hits(row):
-            return jnp.where(code == pqk[row : row + 1, :].astype(BF16), one, none)
-
-        total = code_sums(cent_hits, half, cols, NT)
+        total = cent_sums(1, half)
         part = pl.ds(half * 16, 16)
         comb[part] = (book[half * KSUB : (half + 1) * KSUB, :] - total).reshape(16, 2, 8, 128)
         pair = copy_to(
@@ -367,7 +380,7 @@
         pairs[half].wait()
         sib[part] = sib[part] + comb[part, core]
         send_tiles(half)
-    each_peer(me, send_vec, V2, V3)
+    send_vecs(V2, V3)
     mine = lax.rem(y + z // 2, 2) * 16 + y * 2 + block
     sums_here = lax.rem(z, 2) == core
 
@@ -390,10 +403,11 @@
                 tile, gathered.at[core, mine], gs_sem, gr_sem, lists=peer
             ).start()
 
-        for dy, dz in FAR_FIRST[:-1]:
+        for dy, dz in FAR_FIRST:
             send_sum(rows[dy] + places[dz] + core)
 
-    each_peer(me, send_vec, V3, 8)
+    most = erecv.at[pl.ds(0, N_LISTS - 1)]
+    copy_to(most, most, es_sem, er_sem.at[0], lists=sibling).wait_send()
 
     most = vrecv.at[pl.ds(0, N_LISTS - 1)]
     wait = copy_to(most, most, vs_sem, vr_sem, lists=sibling)
@@ -403,14 +417,20 @@
     vecs = jnp.concatenate(
         [
             jnp.concatenate(
-                [vflat[pl.ds(h * 8 + q, N_LISTS, stride=16), :].astype(BF16) for h in range(2)],
+                [
+                    vflat[pl.ds(part * HALF * 16 + h * 8 + q, HALF, stride=16), :].astype(BF16)
+                    for h in range(2)
+                ],
                 axis=1,
             )
+            for part in range(2)
             for q in range(SLOTS)
         ],
         axis=0,
     )
-    weight = jnp.where(inside, new_scale, 0.0).astype(BF16)
+    weight = jnp.concatenate(
+        [jnp.where(near_inside, near_scale, 0.0), jnp.where(far_inside, far_scale, 0.0)], axis=1
+    ).astype(BF16)
     delta_out[...] = (dot(weight, vecs) - delta_acc[...]).astype(BF16)
 
     @pl.when(sums_here)
@@ -473,7 +493,7 @@
             pltpu.VMEM((LISTS, COLS), F32),
             pltpu.VMEM((N_LISTS * 16, 128), F32),
             pltpu.VMEM((16, N_LISTS * SLOTS), F32),
-            pltpu.VMEM((COLS, N_LISTS * SLOTS), BF16),
+            pltpu.VMEM((2, COLS, HALF * SLOTS), BF16),
             pltpu.VMEM((2 * KSUB, 128), F32),
             pltpu.VMEM((CHIPS // 2, 8, 128), F32),
             pltpu.VMEM((CHIPS // 2, 2, 8, 128), F32),
@@ -482,7 +502,9 @@
             pltpu.VMEM((2, CHIPS // 2, 8, 128), F32),
         ]
         + [pltpu.SemaphoreType.DMA((3,))]
-        + [pltpu.SemaphoreType.DMA] * 11
+        + [pltpu.SemaphoreType.DMA] * 8
+        + [pltpu.SemaphoreType.DMA((2,))]
+        + [pltpu.SemaphoreType.DMA] * 2
         + [pltpu.SemaphoreType.DMA((2,))] * 2
         + [pltpu.SemaphoreType.DMA] * 6
         + [pltpu.SemaphoreType.REGULAR],

time: 49.5 us -> 49.8 us (level)
  no operation moved by 1% of the time
where the time goes in v5:
time: 49.8 us; the launch traced here: 49.6 us
  Pallas kernels  47.6 us (96%)
  local copies, waits for them, and re-layouts  1.41 us (3%)
  between operations  0.64 us (1%)
    pallas_call x1, Pallas kernels, body(): pl.pallas_call(kernel, name='rebuild_window', out_shape=(pltpu.VMEM((LIST...  47.6 us
    unnamed x2, local copies, waits for them, and re-layouts  1.41 us

profile of v5, /device:TPU:1, one launch (start us, length us, event | category | flops | bytes accessed | tf_op | source)
XLA Modules:
  0.0 49.6 jit_solution(13032068868351460116)
XLA Ops:
  0.6 47.6 %rebuild_window.1 = (bf16[512,256]{1,0:T(8,128)(2,1)S(1)}, f32[16,4096]{1,0:T(8,128)S(1)}) custom-call(bf16[128,1024]{1,0:T(8,128)(2,1)} %codes_hbm.1, bf16[1,128]{1,0:T(2,128)(2,1)} %bitcast.5, s32[1,128]{1,0:T(1,128)} %bitcast.6, s32[1,128]{1,0:T(1,128)} %bitcast.7, s32[64,128]{1,0:T(8,128)} %bitcast.4, bf16[512,1024]{1,0:T(8,128)(2,1)} %cent_hbm.1), custom_call_target="tpu_custom_call" | custom-call | tf_op jit(solution)/shard_map/rebuild_window/pallas_call | solution.py:471
  48.2 0.7 %copy.10 = bf16[512,256]{1,0:T(8,128)(2,1)} copy(bf16[512,256]{1,0:T(8,128)(2,1)S(1)} %get-tuple-element.2) | data formatting | bytes 524288
  48.9 0.7 %copy.11 = f32[16,4096]{1,0:T(8,128)} copy(f32[16,4096]{1,0:T(8,128)S(1)} %get-tuple-element.3) | data formatting | bytes 524288

commit v6 on v5

--- a/solution.py
+++ b/solution.py
@@ -23,7 +23,7 @@
 KK = 16
 KSUB = 256
 STACK = 4
-V1, V2, V3 = 40, 40, 63
+V1, V2, V3 = 36, 36, 63
 NT = (((1,), (1,)), ((), ()))
 NN = (((1,), (0,)), ((), ()))
 

time: 49.8 us -> 48.8 us (0.980)
  Pallas kernels: 47.6 us -> 46.6 us
    pallas_call x1, Pallas kernels: 47.6 us -> 46.6 us  [body(): pl.pallas_call(kernel, name='rebuild_window', out_shape=(pltpu.VMEM((LIST...]
where the time goes in v6:
time: 48.8 us; the launch traced here: 48.6 us
  Pallas kernels  46.6 us (95%)
  local copies, waits for them, and re-layouts  1.41 us (3%)
  between operations  0.64 us (1%)
    pallas_call x1, Pallas kernels, body(): pl.pallas_call(kernel, name='rebuild_window', out_shape=(pltpu.VMEM((LIST...  46.6 us
    unnamed x2, local copies, waits for them, and re-layouts  1.41 us

profile of v6, /device:TPU:1, one launch (start us, length us, event | category | flops | bytes accessed | tf_op | source)
XLA Modules:
  0.0 48.6 jit_solution(1541728239144611830)
XLA Ops:
  0.6 46.6 %rebuild_window.1 = (bf16[512,256]{1,0:T(8,128)(2,1)S(1)}, f32[16,4096]{1,0:T(8,128)S(1)}) custom-call(bf16[128,1024]{1,0:T(8,128)(2,1)} %codes_hbm.1, bf16[1,128]{1,0:T(2,128)(2,1)} %bitcast.5, s32[1,128]{1,0:T(1,128)} %bitcast.6, s32[1,128]{1,0:T(1,128)} %bitcast.7, s32[64,128]{1,0:T(8,128)} %bitcast.4, bf16[512,1024]{1,0:T(8,128)(2,1)} %cent_hbm.1), custom_call_target="tpu_custom_call" | custom-call | tf_op jit(solution)/shard_map/rebuild_window/pallas_call | solution.py:471
  47.2 0.7 %copy.10 = bf16[512,256]{1,0:T(8,128)(2,1)} copy(bf16[512,256]{1,0:T(8,128)(2,1)S(1)} %get-tuple-element.2) | data formatting | bytes 524288
  47.9 0.7 %copy.11 = f32[16,4096]{1,0:T(8,128)} copy(f32[16,4096]{1,0:T(8,128)S(1)} %get-tuple-element.3) | data formatting | bytes 524288

commit v7 on v6

--- a/solution.py
+++ b/solution.py
@@ -400,7 +400,7 @@
 
         def send_sum(peer):
             copy_to(
-                tile, gathered.at[core, mine], gs_sem, gr_sem, lists=peer
+                tile, gathered.at[core, mine], gs_sem, gr_sem.at[mine // 16], lists=peer
             ).start()
 
         for dy, dz in FAR_FIRST:
@@ -433,18 +433,24 @@
     ).astype(BF16)
     delta_out[...] = (dot(weight, vecs) - delta_acc[...]).astype(BF16)
 
-    @pl.when(sums_here)
-    def _():
-        most = gathered.at[core, pl.ds(0, CHIPS // 2 - 1)]
-        copy_to(most, most, gs_sem, gr_sem, lists=sibling).wait_recv()
-
-    @pl.when(jnp.logical_not(sums_here))
-    def _():
-        most = gathered.at[core]
-        copy_to(most, most, gs_sem, gr_sem, lists=sibling).wait_recv()
-
-    give = copy_to(gathered.at[core], gathered.at[core], ts_sem, tr_sem, lists=sibling)
-    give.start()
+    gives = []
+    for half in range(2):
+        own_half = sums_here & (mine // 16 == half)
+
+        @pl.when(own_half)
+        def _():
+            most = gathered.at[core, pl.ds(0, 15)]
+            copy_to(most, most, gs_sem, gr_sem.at[half], lists=sibling).wait_recv()
+
+        @pl.when(jnp.logical_not(own_half))
+        def _():
+            most = gathered.at[core, pl.ds(0, 16)]
+            copy_to(most, most, gs_sem, gr_sem.at[half], lists=sibling).wait_recv()
+
+        part = gathered.at[core, pl.ds(half * 16, 16)]
+        give = copy_to(part, part, ts_sem.at[half], tr_sem.at[half], lists=sibling)
+        give.start()
+        gives.append(give)
 
     @pl.when(sums_here)
     def _():
@@ -457,7 +463,8 @@
     def _():
         copy_to(sib, sib, rs_sem, rr_sem, lists=sibling).wait_send()
 
-    give.wait()
+    for give in gives:
+        give.wait()
     for t in range(CHIPS):
         half, block = t // 32, t % 32
         book_out[half * 8 : half * 8 + 8, block * 128 : (block + 1) * 128] = gathered[
@@ -506,7 +513,10 @@
         + [pltpu.SemaphoreType.DMA((2,))]
         + [pltpu.SemaphoreType.DMA] * 2
         + [pltpu.SemaphoreType.DMA((2,))] * 2
-        + [pltpu.SemaphoreType.DMA] * 6
+        + [pltpu.SemaphoreType.DMA] * 2
+        + [pltpu.SemaphoreType.DMA((2,))] * 2
+        + [pltpu.SemaphoreType.DMA]
+        + [pltpu.SemaphoreType.DMA((2,))]
         + [pltpu.SemaphoreType.REGULAR],
         compiler_params=pltpu.CompilerParams(
             collective_id=0, has_side_effects=True, vmem_limit_bytes=56 * 1024 * 1024

time: 48.8 us -> 48.7 us (level)
  no operation moved by 1% of the time
where the time goes in v7:
time: 48.7 us; the launch traced here: 48.6 us
  Pallas kernels  46.5 us (95%)
  local copies, waits for them, and re-layouts  1.41 us (3%)
  between operations  0.64 us (1%)
    pallas_call x1, Pallas kernels, body(): pl.pallas_call(kernel, name='rebuild_window', out_shape=(pltpu.VMEM((LIST...  46.5 us
    unnamed x2, local copies, waits for them, and re-layouts  1.41 us

profile of v7, /device:TPU:1, one launch (start us, length us, event | category | flops | bytes accessed | tf_op | source)
XLA Modules:
  0.0 48.6 jit_solution(3243383142698145010)
XLA Ops:
  0.6 46.5 %rebuild_window.1 = (bf16[512,256]{1,0:T(8,128)(2,1)S(1)}, f32[16,4096]{1,0:T(8,128)S(1)}) custom-call(bf16[128,1024]{1,0:T(8,128)(2,1)} %codes_hbm.1, bf16[1,128]{1,0:T(2,128)(2,1)} %bitcast.5, s32[1,128]{1,0:T(1,128)} %bitcast.6, s32[1,128]{1,0:T(1,128)} %bitcast.7, s32[64,128]{1,0:T(8,128)} %bitcast.4, bf16[512,1024]{1,0:T(8,128)(2,1)} %cent_hbm.1), custom_call_target="tpu_custom_call" | custom-call | tf_op jit(solution)/shard_map/rebuild_window/pallas_call | solution.py:478
  47.2 0.7 %copy.10 = bf16[512,256]{1,0:T(8,128)(2,1)} copy(bf16[512,256]{1,0:T(8,128)(2,1)S(1)} %get-tuple-element.2) | data formatting | bytes 524288
  47.9 0.7 %copy.11 = f32[16,4096]{1,0:T(8,128)} copy(f32[16,4096]{1,0:T(8,128)S(1)} %get-tuple-element.3) | data formatting | bytes 524288
